TPU v7x, 512 devices: a whole 4x8x8 slice. The times are simulated.
512 devices in a mesh: tile: 32 (over x, y), lev: 8 (over z_lo, core), var: 2 (over z_hi).
Axes of the slice: x: 4, y: 8, z: 8 (z_hi: 2, z_lo: 4; z = z_hi * 4 + z_lo), core: 2. Of those that a mesh axis runs over, the one named last changes fastest.
Arguments:
- background: float32 [2, 8, 256, 4096], P('var', 'lev', 'tile'), may hold values from -6 to 6
- norm_factor: float32 [2, 8, 256, 4096], P('var', 'lev', 'tile'), may hold values from 0.05 to 15, as said below
- v_diffusivity: float32 [2, 8, 256, 4096], P('var', None, 'tile', 'lev'), may hold values from 0.5 to 20
- h_diffusivity: float32 [2, 8], P('var', 'lev'), may hold values from 20 to 400
- sea_mask: int32 [8, 256, 4096], P('lev', 'tile'), may hold values 0 or 1
- fold_order: int32 [4096], replicated, may hold values from 0 to 4095, each once
- coupling: float32 [2, 8, 256, 4096], P('var', 'lev', 'tile'), may hold values from -1 to 1
Outputs:
- balanced: float32 [2, 8, 256, 4096], P('var', 'lev', 'tile')
Inputs may be any that keep to these rules, and one draw needn't show every extreme that they name: `norm_factor`: positive normalisation factors.
All inputs are finite; a program needn't handle non-finite values. No bound on the sum of `sea_mask` on one device may be relied on, other than what follows from the above.
Results may differ from a plain program's by a relative error of at most 0.00035.
Values sent between devices are 32-bit elements; how exact they have to be, the bound alone decides.
A program may use at most 64 MiB of HBM per device.

v0:
```python
import jax
import jax.numpy as jnp
from jax import lax
from jax.sharding import PartitionSpec as P

ITERS = 10


def with_halo(shard, sides, width):
    for axis, dim in sides:
        size, length = (lax.axis_size(axis), shard.shape[dim])
        up = [(i, (i + 1) % size) for i in range(size - 1)]
        down = [(j, i) for i, j in up]
        last = lax.slice_in_dim(shard, length - width, length, axis=dim)
        leading = lax.slice_in_dim(shard, 0, width, axis=dim)
        before = lax.ppermute(last, axis, up)
        after = lax.ppermute(leading, axis, down)
        shard = jnp.concatenate([before, shard, after], axis=dim)
    return shard


def swapped_2(value, axis, distance):
    mask = 2**distance
    pairs = [(source, source ^ mask) for source in range(lax.axis_size(axis))]
    return lax.ppermute(value, axis, pairs)


def tridiagonal(rhs, coef):

    def forward(carry, item):
        upper_prev, reduced_prev, coef_prev = carry
        rhs_level, coef_level = item
        pivot = 1.0 + coef_prev + coef_level + coef_prev * upper_prev
        upper_now = -coef_level / pivot
        reduced_now = (rhs_level + coef_prev * reduced_prev) / pivot
        return ((upper_now, reduced_now, coef_level), (upper_now, reduced_now))

    zero_level = jnp.zeros_like(rhs[0])
    final_state, (upper, reduced) = lax.scan(
        forward, (zero_level, zero_level, zero_level), (rhs, coef)
    )

    def backward(following, item):
        upper_now, reduced_now = item
        value = reduced_now - upper_now * following
        return (value, value)

    last_value, solved = lax.scan(backward, zero_level, (upper, reduced), reverse=True)
    return solved


def partner_columns(fold_order):
    swapped = fold_order.reshape(-1, 2)[:, ::-1].reshape(-1)
    return jnp.zeros_like(fold_order).at[fold_order].set(swapped)


def spread(values):
    return values[:, :, None, None]


def per_device(
    background, norm_factor, v_diffusivity, h_diffusivity, sea_mask, fold_order, coupling
):
    scaled = norm_factor * background
    gathered = lax.all_to_all(scaled, "lev", split_axis=3, concat_axis=1, tiled=True)
    solved = tridiagonal(gathered[0], v_diffusivity[0])[None]
    columns = lax.all_to_all(solved, "lev", split_axis=1, concat_axis=3, tiled=True)
    land_free = sea_mask.astype(jnp.float32)[None]
    partner = partner_columns(fold_order)
    is_top = lax.axis_index("tile") == lax.axis_size("tile") - 1

    def squares(residual):
        return lax.psum(jnp.sum(residual * residual, axis=(2, 3)), "tile")

    solution = jnp.zeros_like(columns)
    residual = columns
    direction = columns
    norm_now = squares(residual)
    for iteration in range(ITERS):
        masked = land_free * direction
        padded = with_halo(masked, (("tile", 2),), 1)
        south = padded[:, :, :-2]
        north = padded[:, :, 2:]
        fold_row = masked[:, :, -1][..., partner]
        north = north.at[:, :, -1].add(jnp.where(is_top, fold_row, jnp.zeros_like(fold_row)))
        east = jnp.roll(masked, -1, 3)
        west = jnp.roll(masked, 1, 3)
        laplace = 4.0 * masked - north - south - east - west
        image = direction + spread(h_diffusivity) * land_free * laplace
        step_size = norm_now / lax.psum(jnp.sum(direction * image, axis=(2, 3)), "tile")
        solution = solution + spread(step_size) * direction
        residual = residual - spread(step_size) * image
        norm_next = squares(residual)
        direction = residual + spread(norm_next / norm_now) * direction
        norm_now = norm_next
    other_var = swapped_2(solution, "var", 0)
    return solution + coupling * other_var


def solution(mesh):
    placed = (
        P("var", "lev", "tile", None),
        P("var", "lev", "tile", None),
        P("var", None, "tile", "lev"),
        P("var", "lev"),
        P("lev", "tile", None),
        P(),
        P("var", "lev", "tile", None),
    )
    return jax.shard_map(
        per_device,
        mesh=mesh,
        in_specs=placed,
        out_specs=P("var", "lev", "tile", None),
        check_vma=False,
    )
```

profile of v0, /device:TPU:72, one launch (start us, length us, event | category | flops | bytes accessed | tf_op | source)
XLA Modules:
  0.0 1815.9 jit_solution(8038917067538848912)
XLA Ops:
  4.0 19.3 %reduce.41 = f32[4096,8]{1,0:T(8,128)} reduce(f32[4096,1,1,8]{3,2,1,0:T(1,128)S(1)} %bitcast.171, f32[]{:T(128)} %broadcast.537), dimensions={1,2}, to_apply=%bitcast.124.reduce_sub_computation | reduce | bytes 262148
  26.7 6.9 all-to-all-start
  33.6 5.7 all-to-all-done
  40.2 3.5 reshape.865
  44.3 6.3 while.46
  51.3 4.9 while.47
  56.2 4.4 all-to-all-start.1
  64.2 15.5 scatter_custom_fusion
  80.0 3.8 collective-permute-start
  86.0 23.0 %gather_fusion = f32[4096]{0:T(1024)S(1)} fusion(f32[4096]{0:T(1024)S(1)} %bitcast.156, s32[4096]{0:T(1024)S(1)} %fusion.54), kind=kCustom, calls=%fused_computation | custom fusion | bytes 49152 | tf_op jit(solution)/shard_map/gather | solution.py:84
  111.0 72.4 %all-reduce = (f32[1,1]{1,0:T(1,128)}, f32[1,1]{1,0:T(1,128)}) all-reduce(f32[1,1]{1,0:T(1,128)} %bitcast.7, f32[1,1]{1,0:T(1,128)} %bitcast.15), channel_id=1, replica_groups=mesh['tile'=32,'lev'=8,'var'=2] {'tile'}, use_global_device_ids=true, to_apply=%region_5.6 | all-reduce | flops 2 | bytes 16 | tf_op jit(solution)/shard_map/psum | solution.py:73
  185.3 72.9 %psum.142 = f32[1,1]{1,0:T(1,128)} all-reduce(f32[1,1]{1,0:T(1,128)} %bitcast.17), channel_id=1, replica_groups=mesh['tile'=32,'lev'=8,'var'=2] {'tile'}, use_global_device_ids=true, to_apply=%region_10.11 | all-reduce | flops 1 | bytes 8 | tf_op jit(solution)/shard_map/psum | solution.py:73
  261.7 23.0 %gather_fusion.1 = f32[4096]{0:T(1024)S(1)} fusion(f32[4096]{0:T(1024)S(1)} %bitcast.157, s32[4096]{0:T(1024)S(1)} %fusion.54), kind=kCustom, calls=%fused_computation.1 | custom fusion | bytes 49152 | tf_op jit(solution)/shard_map/gather | solution.py:84
  284.7 3.9 collective-permute-start.2
  291.6 72.2 %psum.143 = f32[1,1]{1,0:T(1,128)} all-reduce(f32[1,1]{1,0:T(1,128)} %bitcast.21), channel_id=1, replica_groups=mesh['tile'=32,'lev'=8,'var'=2] {'tile'}, use_global_device_ids=true, to_apply=%region_12.13 | all-reduce | flops 1 | bytes 8 | tf_op jit(solution)/shard_map/psum | solution.py:90
  365.7 70.2 %psum.144 = f32[1,1]{1,0:T(1,128)} all-reduce(f32[1,1]{1,0:T(1,128)} %bitcast.23), channel_id=1, replica_groups=mesh['tile'=32,'lev'=8,'var'=2] {'tile'}, use_global_device_ids=true, to_apply=%region_14.15 | all-reduce | flops 1 | bytes 8 | tf_op jit(solution)/shard_map/psum | solution.py:73
  439.4 23.0 %gather_fusion.2 = f32[4096]{0:T(1024)S(1)} fusion(f32[4096]{0:T(1024)S(1)} %bitcast.158, s32[4096]{0:T(1024)S(1)} %fusion.54), kind=kCustom, calls=%fused_computation.2 | custom fusion | bytes 49152 | tf_op jit(solution)/shard_map/gather | solution.py:84
  462.4 3.9 collective-permute-start.4
  470.8 72.1 %psum.145 = f32[1,1]{1,0:T(1,128)} all-reduce(f32[1,1]{1,0:T(1,128)} %bitcast.27), channel_id=1, replica_groups=mesh['tile'=32,'lev'=8,'var'=2] {'tile'}, use_global_device_ids=true, to_apply=%region_16.17 | all-reduce | flops 1 | bytes 8 | tf_op jit(solution)/shard_map/psum | solution.py:90
  544.9 70.3 %psum.146 = f32[1,1]{1,0:T(1,128)} all-reduce(f32[1,1]{1,0:T(1,128)} %bitcast.29), channel_id=1, replica_groups=mesh['tile'=32,'lev'=8,'var'=2] {'tile'}, use_global_device_ids=true, to_apply=%region_18.19 | all-reduce | flops 1 | bytes 8 | tf_op jit(solution)/shard_map/psum | solution.py:73
  618.5 23.0 %gather_fusion.3 = f32[4096]{0:T(1024)S(1)} fusion(f32[4096]{0:T(1024)S(1)} %bitcast.159, s32[4096]{0:T(1024)S(1)} %fusion.54), kind=kCustom, calls=%fused_computation.3 | custom fusion | bytes 49152 | tf_op jit(solution)/shard_map/gather | solution.py:84
  641.6 3.9 collective-permute-start.6
  651.2 72.1 %psum.147 = f32[1,1]{1,0:T(1,128)} all-reduce(f32[1,1]{1,0:T(1,128)} %bitcast.33), channel_id=1, replica_groups=mesh['tile'=32,'lev'=8,'var'=2] {'tile'}, use_global_device_ids=true, to_apply=%region_20.21 | all-reduce | flops 1 | bytes 8 | tf_op jit(solution)/shard_map/psum | solution.py:90
  725.3 70.3 %psum.148 = f32[1,1]{1,0:T(1,128)} all-reduce(f32[1,1]{1,0:T(1,128)} %bitcast.35), channel_id=1, replica_groups=mesh['tile'=32,'lev'=8,'var'=2] {'tile'}, use_global_device_ids=true, to_apply=%region_22.23 | all-reduce | flops 1 | bytes 8 | tf_op jit(solution)/shard_map/psum | solution.py:73
  798.9 23.0 %gather_fusion.4 = f32[4096]{0:T(1024)S(1)} fusion(f32[4096]{0:T(1024)S(1)} %bitcast.160, s32[4096]{0:T(1024)S(1)} %fusion.54), kind=kCustom, calls=%fused_computation.4 | custom fusion | bytes 49152 | tf_op jit(solution)/shard_map/gather | solution.py:84
  822.0 3.9 collective-permute-start.8
  831.6 72.1 %psum.149 = f32[1,1]{1,0:T(1,128)} all-reduce(f32[1,1]{1,0:T(1,128)} %bitcast.39), channel_id=1, replica_groups=mesh['tile'=32,'lev'=8,'var'=2] {'tile'}, use_global_device_ids=true, to_apply=%region_24.25 | all-reduce | flops 1 | bytes 8 | tf_op jit(solution)/shard_map/psum | solution.py:90
  905.6 70.3 %psum.150 = f32[1,1]{1,0:T(1,128)} all-reduce(f32[1,1]{1,0:T(1,128)} %bitcast.41), channel_id=1, replica_groups=mesh['tile'=32,'lev'=8,'var'=2] {'tile'}, use_global_device_ids=true, to_apply=%region_26.27 | all-reduce | flops 1 | bytes 8 | tf_op jit(solution)/shard_map/psum | solution.py:73
  979.2 23.0 %gather_fusion.5 = f32[4096]{0:T(1024)S(1)} fusion(f32[4096]{0:T(1024)S(1)} %bitcast.161, s32[4096]{0:T(1024)S(1)} %fusion.54), kind=kCustom, calls=%fused_computation.5 | custom fusion | bytes 49152 | tf_op jit(solution)/shard_map/gather | solution.py:84
  1002.3 3.9 collective-permute-start.10
  1011.9 72.1 %psum.151 = f32[1,1]{1,0:T(1,128)} all-reduce(f32[1,1]{1,0:T(1,128)} %bitcast.45), channel_id=1, replica_groups=mesh['tile'=32,'lev'=8,'var'=2] {'tile'}, use_global_device_ids=true, to_apply=%region_28.29 | all-reduce | flops 1 | bytes 8 | tf_op jit(solution)/shard_map/psum | solution.py:90
  1085.9 70.3 %psum.152 = f32[1,1]{1,0:T(1,128)} all-reduce(f32[1,1]{1,0:T(1,128)} %bitcast.47), channel_id=1, replica_groups=mesh['tile'=32,'lev'=8,'var'=2] {'tile'}, use_global_device_ids=true, to_apply=%region_30.31 | all-reduce | flops 1 | bytes 8 | tf_op jit(solution)/shard_map/psum | solution.py:73
  1159.6 23.0 %gather_fusion.6 = f32[4096]{0:T(1024)S(1)} fusion(f32[4096]{0:T(1024)S(1)} %bitcast.162, s32[4096]{0:T(1024)S(1)} %fusion.54), kind=kCustom, calls=%fused_computation.6 | custom fusion | bytes 49152 | tf_op jit(solution)/shard_map/gather | solution.py:84
  1182.6 3.9 collective-permute-start.12
  1192.2 72.1 %psum.153 = f32[1,1]{1,0:T(1,128)} all-reduce(f32[1,1]{1,0:T(1,128)} %bitcast.51), channel_id=1, replica_groups=mesh['tile'=32,'lev'=8,'var'=2] {'tile'}, use_global_device_ids=true, to_apply=%region_32.33 | all-reduce | flops 1 | bytes 8 | tf_op jit(solution)/shard_map/psum | solution.py:90
  1266.4 70.2 %psum.154 = f32[1,1]{1,0:T(1,128)} all-reduce(f32[1,1]{1,0:T(1,128)} %bitcast.53), channel_id=1, replica_groups=mesh['tile'=32,'lev'=8,'var'=2] {'tile'}, use_global_device_ids=true, to_apply=%region_34.35 | all-reduce | flops 1 | bytes 8 | tf_op jit(solution)/shard_map/psum | solution.py:73
  1340.0 23.0 %gather_fusion.7 = f32[4096]{0:T(1024)S(1)} fusion(f32[4096]{0:T(1024)S(1)} %bitcast.163, s32[4096]{0:T(1024)S(1)} %fusion.54), kind=kCustom, calls=%fused_computation.7 | custom fusion | bytes 49152 | tf_op jit(solution)/shard_map/gather | solution.py:84
  1363.0 3.9 collective-permute-start.14
  1372.7 72.1 %psum.155 = f32[1,1]{1,0:T(1,128)} all-reduce(f32[1,1]{1,0:T(1,128)} %bitcast.57), channel_id=1, replica_groups=mesh['tile'=32,'lev'=8,'var'=2] {'tile'}, use_global_device_ids=true, to_apply=%region_36.37 | all-reduce | flops 1 | bytes 8 | tf_op jit(solution)/shard_map/psum | solution.py:90
  1446.7 70.3 %psum.156 = f32[1,1]{1,0:T(1,128)} all-reduce(f32[1,1]{1,0:T(1,128)} %bitcast.59), channel_id=1, replica_groups=mesh['tile'=32,'lev'=8,'var'=2] {'tile'}, use_global_device_ids=true, to_apply=%region_38.39 | all-reduce | flops 1 | bytes 8 | tf_op jit(solution)/shard_map/psum | solution.py:73
  1520.4 23.0 %gather_fusion.8 = f32[4096]{0:T(1024)S(1)} fusion(f32[4096]{0:T(1024)S(1)} %bitcast.164, s32[4096]{0:T(1024)S(1)} %fusion.54), kind=kCustom, calls=%fused_computation.8 | custom fusion | bytes 49152 | tf_op jit(solution)/shard_map/gather | solution.py:84
  1543.4 3.9 collective-permute-start.16
  1553.0 72.1 %psum.157 = f32[1,1]{1,0:T(1,128)} all-reduce(f32[1,1]{1,0:T(1,128)} %bitcast.63), channel_id=1, replica_groups=mesh['tile'=32,'lev'=8,'var'=2] {'tile'}, use_global_device_ids=true, to_apply=%region_40.41 | all-reduce | flops 1 | bytes 8 | tf_op jit(solution)/shard_map/psum | solution.py:90
  1627.1 70.1 %psum.158 = f32[1,1]{1,0:T(1,128)} all-reduce(f32[1,1]{1,0:T(1,128)} %bitcast.65), channel_id=1, replica_groups=mesh['tile'=32,'lev'=8,'var'=2] {'tile'}, use_global_device_ids=true, to_apply=%region_42.43 | all-reduce | flops 1 | bytes 8 | tf_op jit(solution)/shard_map/psum | solution.py:73
  1700.6 23.0 %gather_fusion.9 = f32[4096]{0:T(1024)S(1)} fusion(f32[4096]{0:T(1024)S(1)} %bitcast.155, s32[4096]{0:T(1024)S(1)} %fusion.54), kind=kCustom, calls=%fused_computation.9 | custom fusion | bytes 49152 | tf_op jit(solution)/shard_map/gather | solution.py:84
  1723.7 4.0 collective-permute-start.18
  1730.7 72.1 %psum.159 = f32[1,1]{1,0:T(1,128)} all-reduce(f32[1,1]{1,0:T(1,128)} %bitcast.69), channel_id=1, replica_groups=mesh['tile'=32,'lev'=8,'var'=2] {'tile'}, use_global_device_ids=true, to_apply=%region_44.45 | all-reduce | flops 1 | bytes 8 | tf_op jit(solution)/shard_map/psum | solution.py:90
  1804.1 8.2 collective-permute-start.20
  (192 shorter events, 100.0 us)
Async XLA Ops:
  26.7 12.6 all-to-all-start
  43.7 16.9 copy-start.3
  56.2 23.5 %all-to-all-start.1 = ((f32[1,8,8,512]{3,2,0,1:T(8,128)}), f32[1,8,8,512]{3,2,0,1:T(8,128)S(1)}, u32[]{:S(2)}, u32[]{:S(2)}) async-start(f32[1,8,8,512]{3,2,0,1:T(8,128)} %bitcast.4), calls=%async_computation.1 | async-start | bytes 262144 | tf_op jit(solution)/shard_map/all_to_all | solution.py:67
  60.6 19.2 %copy-start = (s32[1,8,4096]{2,1,0:T(8,128)S(1)}, s32[1,8,4096]{2,1,0:T(8,128)}, u32[]{:S(2)}) copy-start(s32[1,8,4096]{2,1,0:T(8,128)} %param.35) | copy-start | bytes 393220
  80.0 29.8 %collective-permute-start = (f32[1,1,1,4096]{3,2,1,0:T(1,128)S(1)}, f32[1,1,1,4096]{3,2,1,0:T(1,128)S(1)}, u32[]{:S(2)}, u32[]{:S(2)}) collective-permute-start(f32[1,1,1,4096]{3,2,1,0:T(1,128)S(1)} %get-tuple-element.458), channel_id=1, source_target_pairs={{16,0},{32,16},{48,32},{64,48},{80,64},{96,80},{112,96},{128,112},... | collective-permute-start | bytes 49160 | tf_op jit(solution)/shard_map/ppermute | solution.py:17
  83.8 26.5 %collective-permute-start.1 = (f32[1,1,1,4096]{3,2,1,0:T(1,128)S(1)}, f32[1,1,1,4096]{3,2,1,0:T(1,128)S(1)}, u32[]{:S(2)}, u32[]{:S(2)}) collective-permute-start(f32[1,1,1,4096]{3,2,1,0:T(1,128)S(1)} %get-tuple-element.459), channel_id=1, source_target_pairs={{0,16},{16,32},{32,48},{48,64},{64,80},{80,96},{96,112},{112,128},... | collective-permute-start | bytes 49160 | tf_op jit(solution)/shard_map/ppermute | solution.py:16
  259.8 31.1 %collective-permute-start.3 = (f32[1,1,1,4096]{3,2,1,0:T(1,128)S(1)}, f32[1,1,1,4096]{3,2,1,0:T(1,128)S(1)}, u32[]{:S(2)}, u32[]{:S(2)}) collective-permute-start(f32[1,1,1,4096]{3,2,1,0:T(1,128)S(1)} %get-tuple-element.453), channel_id=1, source_target_pairs={{0,16},{16,32},{32,48},{48,64},{64,80},{80,96},{96,112},{112,128},... | collective-permute-start | bytes 49160 | tf_op jit(solution)/shard_map/ppermute | solution.py:16
  284.7 5.6 collective-permute-start.2
  437.4 31.1 %collective-permute-start.5 = (f32[1,1,1,4096]{3,2,1,0:T(1,128)S(1)}, f32[1,1,1,4096]{3,2,1,0:T(1,128)S(1)}, u32[]{:S(2)}, u32[]{:S(2)}) collective-permute-start(f32[1,1,1,4096]{3,2,1,0:T(1,128)S(1)} %get-tuple-element.447), channel_id=1, source_target_pairs={{0,16},{16,32},{32,48},{48,64},{64,80},{80,96},{96,112},{112,128},... | collective-permute-start | bytes 49160 | tf_op jit(solution)/shard_map/ppermute | solution.py:16
  462.4 5.6 collective-permute-start.4
  468.5 0.7 copy-start.1
  616.6 32.9 %collective-permute-start.7 = (f32[1,1,1,4096]{3,2,1,0:T(1,128)S(1)}, f32[1,1,1,4096]{3,2,1,0:T(1,128)S(1)}, u32[]{:S(2)}, u32[]{:S(2)}) collective-permute-start(f32[1,1,1,4096]{3,2,1,0:T(1,128)S(1)} %get-tuple-element.441), channel_id=1, source_target_pairs={{0,16},{16,32},{32,48},{48,64},{64,80},{80,96},{96,112},{112,128},... | collective-permute-start | bytes 49160 | tf_op jit(solution)/shard_map/ppermute | solution.py:16
  641.6 5.6 collective-permute-start.6
  797.0 32.9 %collective-permute-start.9 = (f32[1,1,1,4096]{3,2,1,0:T(1,128)S(1)}, f32[1,1,1,4096]{3,2,1,0:T(1,128)S(1)}, u32[]{:S(2)}, u32[]{:S(2)}) collective-permute-start(f32[1,1,1,4096]{3,2,1,0:T(1,128)S(1)} %get-tuple-element.435), channel_id=1, source_target_pairs={{0,16},{16,32},{32,48},{48,64},{64,80},{80,96},{96,112},{112,128},... | collective-permute-start | bytes 49160 | tf_op jit(solution)/shard_map/ppermute | solution.py:16
  822.0 5.6 collective-permute-start.8
  977.3 32.9 %collective-permute-start.11 = (f32[1,1,1,4096]{3,2,1,0:T(1,128)S(1)}, f32[1,1,1,4096]{3,2,1,0:T(1,128)S(1)}, u32[]{:S(2)}, u32[]{:S(2)}) collective-permute-start(f32[1,1,1,4096]{3,2,1,0:T(1,128)S(1)} %get-tuple-element.429), channel_id=1, source_target_pairs={{0,16},{16,32},{32,48},{48,64},{64,80},{80,96},{96,112},{112,128},... | collective-permute-start | bytes 49160 | tf_op jit(solution)/shard_map/ppermute | solution.py:16
  1002.3 5.6 collective-permute-start.10
  1157.6 32.9 %collective-permute-start.13 = (f32[1,1,1,4096]{3,2,1,0:T(1,128)S(1)}, f32[1,1,1,4096]{3,2,1,0:T(1,128)S(1)}, u32[]{:S(2)}, u32[]{:S(2)}) collective-permute-start(f32[1,1,1,4096]{3,2,1,0:T(1,128)S(1)} %get-tuple-element.423), channel_id=1, source_target_pairs={{0,16},{16,32},{32,48},{48,64},{64,80},{80,96},{96,112},{112,128},... | collective-permute-start | bytes 49160 | tf_op jit(solution)/shard_map/ppermute | solution.py:16
  1182.6 5.6 collective-permute-start.12
  1338.0 32.9 %collective-permute-start.15 = (f32[1,1,1,4096]{3,2,1,0:T(1,128)S(1)}, f32[1,1,1,4096]{3,2,1,0:T(1,128)S(1)}, u32[]{:S(2)}, u32[]{:S(2)}) collective-permute-start(f32[1,1,1,4096]{3,2,1,0:T(1,128)S(1)} %get-tuple-element.417), channel_id=1, source_target_pairs={{0,16},{16,32},{32,48},{48,64},{64,80},{80,96},{96,112},{112,128},... | collective-permute-start | bytes 49160 | tf_op jit(solution)/shard_map/ppermute | solution.py:16
  1363.0 5.6 collective-permute-start.14
  1518.4 32.9 %collective-permute-start.17 = (f32[1,1,1,4096]{3,2,1,0:T(1,128)S(1)}, f32[1,1,1,4096]{3,2,1,0:T(1,128)S(1)}, u32[]{:S(2)}, u32[]{:S(2)}) collective-permute-start(f32[1,1,1,4096]{3,2,1,0:T(1,128)S(1)} %get-tuple-element.411), channel_id=1, source_target_pairs={{0,16},{16,32},{32,48},{48,64},{64,80},{80,96},{96,112},{112,128},... | collective-permute-start | bytes 49160 | tf_op jit(solution)/shard_map/ppermute | solution.py:16
  1543.4 5.6 collective-permute-start.16
  1698.7 31.2 %collective-permute-start.19 = (f32[1,1,1,4096]{3,2,1,0:T(1,128)S(1)}, f32[1,1,1,4096]{3,2,1,0:T(1,128)S(1)}, u32[]{:S(2)}, u32[]{:S(2)}) collective-permute-start(f32[1,1,1,4096]{3,2,1,0:T(1,128)S(1)} %get-tuple-element.405), channel_id=1, source_target_pairs={{0,16},{16,32},{32,48},{48,64},{64,80},{80,96},{96,112},{112,128},... | collective-permute-start | bytes 49160 | tf_op jit(solution)/shard_map/ppermute | solution.py:16
  1723.7 91.6 %copy-start.2 = (f32[1,1,8,4096]{3,2,1,0:T(8,128)S(1)}, f32[1,1,8,4096]{3,2,1,0:T(8,128)}, u32[]{:S(2)}) copy-start(f32[1,1,8,4096]{3,2,1,0:T(8,128)} %param.37) | copy-start | bytes 393220
  1723.7 5.8 collective-permute-start.18
  1804.1 11.2 collective-permute-start.20
where the time goes:
time: 1820 us
  blocking collectives  1360 us (75%)
  local copies, waits for them, and re-layouts  274 us (15%)
  starting transfers between devices  78.2 us (4%)
  other arithmetic  57.9 us (3%)
  between operations  26.1 us (1%)
  waiting for transfers between devices  23.3 us (1%)
    psum x10, blocking collectives, squares(): return lax.psum(jnp.sum(residual * residual, axis=(2, 3)), 'tile')  707 us
    psum x9, blocking collectives, per_device(): lax.psum(jnp.sum(direction * image, axis=(2, 3)), 'tile')  649 us
    gather x10, local copies, waits for them, and re-layouts, per_device(): fold_row = masked[:, :, -1][..., partner]  230 us
    ppermute x10, starting transfers between devices, with_halo(): after = lax.ppermute(leading, axis, down)  39.2 us
  transfers between devices with their start and end apart: 23, of which 11 were waited for; matrix products, arithmetic and copies ran while one was open for 15% of the time, Pallas kernels for 0%

commit v1 on v0

v1 whole, which is shorter than its diff:
```python
import functools

import jax
import jax.numpy as jnp
from jax import lax
from jax.experimental import pallas as pl
from jax.experimental.pallas import tpu as pltpu
from jax.sharding import PartitionSpec as P

MESH = pl.DeviceIdType.MESH
STEPS = 5
SHIFTS = (0.0, 6.0, 3.0, 7.0, 1.5)
ROWS = 8
PAD = 128
OWN = slice(16, 24)


def starts_of(chains):
    starts, at = [], 0
    for length in chains:
        starts.append(at)
        at += length
    return starts, at


def gram_message(vectors, columns):
    count = len(vectors)
    pairs = [(i, j) for i in range(count) for j in range(i, count)]
    lane = lax.broadcasted_iota(jnp.int32, (8, 128), 1)
    message = jnp.zeros((8, 128), jnp.float32)
    for at in range(0, len(pairs), 22):
        group = pairs[at : at + 22]
        used = sorted({i for pair in group for i in pair})

        def body(block, sums, group=group, used=used):
            held = {i: vectors[i](block) for i in used}
            return tuple(total + held[i] * held[j] for total, (i, j) in zip(sums, group))

        zeros = tuple(jnp.zeros((8, 128), jnp.float32) for _ in group)
        sums = lax.fori_loop(0, columns // 128, body, zeros, unroll=8)
        for total, (i, j) in zip(sums, group):
            here = (lane == count * i + j) | (lane == count * j + i)
            message = jnp.where(here, jnp.sum(total, axis=1, keepdims=True), message)
    return jnp.sum(message, axis=0, keepdims=True)


def coefficient_cg(totals, chains, diffusivity, steps, last):
    starts, count = starts_of(chains)
    shape = (16, 128)
    row = lax.broadcasted_iota(jnp.int32, shape, 0)
    lane = lax.broadcasted_iota(jnp.int32, shape, 1)
    gram = jnp.zeros(shape, jnp.float32)
    for i in range(count):
        line = totals if i == 0 else pltpu.roll(totals, 128 - count * i, 1)
        gram = jnp.where((row == i) & (lane < count), jnp.broadcast_to(line, shape), gram)

    def coefficients(index):
        same = jnp.zeros(shape, jnp.float32)
        step_up = jnp.zeros(shape, jnp.float32)
        for start, length in zip(starts, chains):
            for j in range(length - 1):
                same = jnp.where(index == start + j, 1.0 + diffusivity * SHIFTS[j], same)
                step_up = jnp.where(index == start + j + 1, 4.0 * diffusivity, step_up)
        return same, step_up

    same_row, up_row = coefficients(lane)
    same_col, up_col = coefficients(row)

    def total(value):
        return jnp.sum(jnp.sum(value, axis=0, keepdims=True), axis=1, keepdims=True)

    one, zero = jnp.ones(shape, jnp.float32), jnp.zeros(shape, jnp.float32)
    d_row, d_col = jnp.where(lane == 0, one, zero), jnp.where(row == 0, one, zero)
    first = starts[-1]
    r_row, r_col = jnp.where(lane == first, one, zero), jnp.where(row == first, one, zero)
    x_col = zero
    norm_now = total(r_col * gram * r_row)
    for step in range(steps):
        image_row = same_row * d_row + up_row * pltpu.roll(d_row, 1, 1)
        energy = total(d_col * gram * image_row)
        size = jnp.where(energy > 0, jnp.minimum(norm_now / energy, 1.0), 0.0)
        x_col = x_col + size * d_col
        if last and step == steps - 1:
            break
        image_col = same_col * d_col + up_col * pltpu.roll(d_col, 1, 0)
        r_row = r_row - size * image_row
        r_col = r_col - size * image_col
        norm_next = jnp.maximum(total(r_col * gram * r_row), 0.0)
        ratio = jnp.where(norm_now > 0, norm_next / norm_now, 0.0)
        d_row = r_row + ratio * d_row
        d_col = r_col + ratio * d_col
        norm_now = norm_next
    return x_col, r_col, d_col


def operator(source, target, quarter_mask, columns, shift, rows, loaded, width=512):
    (low, high), (from_row, to_row) = rows, loaded
    inside = slice(low - from_row, high - from_row)
    span = width + 2 * PAD

    def body(chunk, carry):
        at = pl.multiple_of(chunk * width, width)
        wide = source[from_row:to_row, pl.ds(at, span)]
        center = wide[:, PAD : PAD + width]
        middle = wide[inside]
        east = pltpu.roll(middle, span - 1, 1)[:, PAD : PAD + width]
        west = pltpu.roll(middle, 1, 1)[:, PAD : PAD + width]
        north = pltpu.roll(center, to_row - from_row - 1, 0)[inside]
        south = pltpu.roll(center, 1, 0)[inside]
        here = center[inside]
        laplace = 4.0 * here - ((north + south) + (east + west))
        value = quarter_mask[low:high, pl.ds(at, width)] * laplace
        if shift:
            value = value - (0.25 * shift) * here
        target[low:high, pl.ds(at + PAD, width)] = value
        return carry

    lax.fori_loop(0, columns // width, body, 0, unroll=True)
    wrap(target, rows, columns)


def wrap(target, rows, columns):
    low, high = rows
    target[low:high, 0:PAD] = target[low:high, columns : columns + PAD]
    target[low:high, columns + PAD : columns + 2 * PAD] = target[low:high, PAD : 2 * PAD]


def kernel(
    background, norm_factor, v_diffusivity, h_diffusivity, sea_mask, fold_order,
    solved_out, other_out,
    bg, nf, vd, mask_in, fold_in, scaled, rhs, solved, inverse, below, upper,
    field, quarter_mask, v_chain, p_chain, r_chain, masked_p, masked_r, p_own, r_own,
    partner_row, partner_lane, folded, message, received, result, coef,
    load_sem, there_send, there_recv, back_send, back_recv,
    halo_send, halo_recv, mask_send, mask_recv, sum_send, sum_recv, last_send, last_recv, last_local,
):
    tile, lev, var = (lax.axis_index(a) for a in ("tile", "lev", "var"))
    tiles, levels = lax.axis_size("tile"), lax.axis_size("lev")
    columns = bg.shape[1]
    part = columns // levels
    top = tiles - 1
    blocks = columns // 128
    f32 = jnp.float32

    loads = [
        pltpu.make_async_copy(source, target, load_sem.at[i])
        for i, (source, target) in enumerate(
            ((background, bg), (norm_factor, nf), (sea_mask, mask_in), (v_diffusivity, vd), (fold_order, fold_in))
        )
    ]
    for load in loads:
        load.start()
    for buffer in (field, quarter_mask):
        for low in (0, 8, 24, 32):
            buffer[low : low + 8, :] = jnp.zeros((8, columns), f32)
    barrier = pltpu.get_barrier_semaphore()

    def greet_level(d, carry):
        pl.semaphore_signal(barrier, inc=1, device_id={"lev": lax.rem(lev + d, levels)}, device_id_type=MESH)
        return carry

    def greet_tile(d, carry):
        pl.semaphore_signal(barrier, inc=1, device_id={"tile": lax.rem(tile + d, tiles)}, device_id_type=MESH)
        return carry

    lax.fori_loop(1, levels, greet_level, 0)
    lax.fori_loop(1, tiles, greet_tile, 0)
    pl.semaphore_signal(barrier, inc=1, device_id={"var": 1 - var}, device_id_type=MESH)
    loads[0].wait()
    loads[1].wait()
    scaled[...] = nf[...] * bg[...]
    loads[2].wait()
    quarter_mask[OWN, :] = 0.25 * mask_in[...].astype(f32)
    pl.semaphore_wait(barrier, (levels - 1) + (tiles - 1) + 1)

    def send_there(d, carry):
        to = lax.rem(lev + d, levels)
        pltpu.make_async_remote_copy(
            src_ref=scaled.at[:, pl.ds(pl.multiple_of(to * part, part), part)],
            dst_ref=rhs.at[lev],
            send_sem=there_send,
            recv_sem=there_recv,
            device_id={"lev": to},
            device_id_type=MESH,
        ).start()
        return carry

    lax.fori_loop(1, levels, send_there, 0)
    rhs[lev] = scaled[:, pl.ds(pl.multiple_of(lev * part, part), part)]

    sides = ((16, 24, 8, 1), (16, 24, 24, -1), (22, 24, 6, 2), (16, 18, 32, -2))

    def reached(distance):
        return tile + distance <= top if distance > 0 else tile + distance >= 0

    def halo_copies(buffer, send, recv, at, width):
        for side, (low, high, land, distance) in enumerate(sides):

            @pl.when(reached(distance))
            def _(side=side, low=low, high=high, land=land, distance=distance):
                pltpu.make_async_remote_copy(
                    src_ref=buffer.at[low:high, pl.ds(at, width)],
                    dst_ref=buffer.at[land : land + high - low, pl.ds(at, width)],
                    send_sem=send.at[side],
                    recv_sem=recv.at[side],
                    device_id={"tile": tile + distance},
                    device_id_type=MESH,
                ).start()

    def halo_wait(buffer, sem, receive):
        for side, (low, high, land, distance) in enumerate(sides):

            @pl.when(reached(-distance if receive else distance))
            def _(side=side, low=low, high=high, land=land):
                at = slice(land, land + high - low) if receive else slice(low, high)
                pltpu.make_async_copy(buffer.at[at, :], buffer.at[at, :], sem.at[side]).wait()

    halo_copies(quarter_mask, mask_send, mask_recv, 0, columns)

    loads[3].wait()
    above = jnp.zeros((ROWS, part), f32)
    upper_now = above
    for level in range(levels):
        coefficient = vd[level]
        inv = 1.0 / (1.0 + above + coefficient + above * upper_now)
        inverse[level] = inv
        below[level] = above * inv
        upper_now = -coefficient * inv
        upper[level] = upper_now
        above = coefficient

    loads[4].wait()

    @pl.when(tile >= top - 1)
    def _():
        order = fold_in[...]
        lane = lax.broadcasted_iota(jnp.int32, (1, columns), 1)
        mate = jnp.where(lane % 2 == 0, pltpu.roll(order, columns - 1, 1), pltpu.roll(order, 1, 1))
        row_hot = lax.broadcasted_iota(jnp.int32, (blocks, columns), 0) == order // 128
        lane_hot = lax.broadcasted_iota(jnp.int32, (128, columns), 0) == order % 128
        high = jnp.where(row_hot, (mate // 64).astype(f32), 0.0)
        low = jnp.where(row_hot, (mate % 64).astype(f32), 0.0)
        left = jnp.concatenate([high, low], axis=0).astype(jnp.bfloat16)
        right = jnp.where(lane_hot, 1.0, 0.0).astype(jnp.bfloat16)
        found = lax.dot_general(left, right, (((1,), (1,)), ((), ())), preferred_element_type=f32)
        partner = 64 * found[:blocks].astype(jnp.int32) + found[blocks:].astype(jnp.int32)
        partner_row[...] = partner // 128
        partner_lane[...] = partner % 128

    pltpu.make_async_copy(rhs.at[0 : levels - 1], rhs.at[0 : levels - 1], there_recv).wait()
    reduced = jnp.zeros((ROWS, part), f32)
    for level in range(levels):
        reduced = rhs[level] * inverse[level] + below[level] * reduced
        solved[level] = reduced
    value = jnp.zeros((ROWS, part), f32)
    for level in reversed(range(levels)):
        value = solved[level] - upper[level] * value
        solved[level] = value

    my_columns = pl.multiple_of(lev * part, part)

    def send_back(d, carry):
        to = lax.rem(lev + d, levels)
        pltpu.make_async_remote_copy(
            src_ref=solved.at[to],
            dst_ref=field.at[OWN, pl.ds(my_columns, part)],
            send_sem=back_send,
            recv_sem=back_recv.at[d],
            device_id={"lev": to},
            device_id_type=MESH,
        ).start()
        return carry

    lax.fori_loop(1, levels, send_back, 0)
    field[OWN, pl.ds(my_columns, part)] = solved[lev]
    halo_copies(field, halo_send, halo_recv, my_columns, part)

    def pass_on(d, carry):
        at = pl.multiple_of(lax.rem(lev + levels - d, levels) * part, part)
        here = field.at[OWN, pl.ds(at, part)]
        pltpu.make_async_copy(here, here, back_recv.at[d]).wait()
        halo_copies(field, halo_send, halo_recv, at, part)
        return carry

    lax.fori_loop(1, levels, pass_on, 0)

    def fold(buffer, last_row):
        sums = tuple(jnp.zeros((8, 128), f32) for _ in range(blocks // 8))

        def pick(block, sums):
            at = pl.multiple_of(PAD + block * 128, 128)
            line = jnp.broadcast_to(buffer[last_row : last_row + 1, pl.ds(at, 128)], (8, 128))
            chosen = []
            for q, now in enumerate(sums):
                rows = slice(8 * q, 8 * q + 8)
                moved = jnp.take_along_axis(line, partner_lane[rows, :], axis=1)
                chosen.append(jnp.where(partner_row[rows, :] == block, moved, now))
            return tuple(chosen)

        sums = lax.fori_loop(0, blocks, pick, sums, unroll=True)
        for q, now in enumerate(sums):
            folded[8 * q : 8 * q + 8, :] = now
        for block in range(blocks):
            buffer[last_row + 1 : last_row + 2, PAD + block * 128 : PAD + block * 128 + 128] = folded[block : block + 1, :]

    def fold_top(buffer):
        @pl.when(tile == top)
        def _():
            fold(buffer, 23)

    def fold_next(buffer):
        @pl.when(tile == top - 1)
        def _():
            fold(buffer, 31)

    halo_wait(quarter_mask, mask_recv, True)
    halo_wait(field, halo_recv, True)
    masked = masked_p

    def apply_mask(chunk, carry):
        at = pl.multiple_of(chunk * 512, 512)
        masked[:, pl.ds(at + PAD, 512)] = 4.0 * quarter_mask[:, pl.ds(at, 512)] * field[:, pl.ds(at, 512)]
        return carry

    lax.fori_loop(0, columns // 512, apply_mask, 0, unroll=True)
    wrap(masked, (0, 40), columns)
    source = masked
    for j in range(STEPS):
        fold_top(source)
        if j < 2:
            fold_next(source)
        rows, loaded = ((0, 40), (0, 40)) if j == 0 else ((8, 32), (0, 40) if j == 1 else (8, 32))
        operator(source, v_chain[j], quarter_mask, columns, SHIFTS[j], rows, loaded)
        source = v_chain[j]

    def own_of(buffer, pad):
        rows = OWN if buffer.shape[0] == 40 else slice(0, 8)
        return lambda block: buffer[rows, pl.ds(pl.multiple_of(block * 128 + pad, 128), 128)]

    def reduce_over_tiles(index):
        def send(d, carry):
            pltpu.make_async_remote_copy(
                src_ref=message.at[index],
                dst_ref=received.at[index, tile],
                send_sem=sum_send.at[index],
                recv_sem=sum_recv.at[index],
                device_id={"tile": lax.rem(tile + d, tiles)},
                device_id_type=MESH,
            ).start()
            return carry

        lax.fori_loop(1, tiles, send, 0)

    def sum_over_tiles(index):
        others = received.at[index, 0 : tiles - 1]
        pltpu.make_async_copy(others, others, sum_recv.at[index]).wait()
        return jnp.sum(received[index], axis=0)

    shared = gram_message([own_of(field, 0)] + [own_of(v, PAD) for v in v_chain], columns)
    message[0] = shared
    received[0, tile] = shared
    reduce_over_tiles(0)
    diffusivity = h_diffusivity[0, 0]
    x_col, r_col, d_col = coefficient_cg(sum_over_tiles(0), (STEPS + 1,), diffusivity, STEPS, False)
    coef[0:16, :] = x_col
    coef[16:32, :] = r_col
    coef[32:48, :] = d_col

    def next_round(block, carry):
        at = pl.multiple_of(block * 128, 128)
        rows = slice(8, 32)
        held = [field[rows, pl.ds(at, 128)]] + [v[rows, pl.ds(at + PAD, 128)] for v in v_chain]
        residual = sum(coef[16 + j : 17 + j, :] * held[j] for j in range(STEPS + 1))
        direction = sum(coef[32 + j : 33 + j, :] * held[j] for j in range(STEPS + 1))
        mask = 4.0 * quarter_mask[rows, pl.ds(at, 128)]
        masked_r[rows, pl.ds(at + PAD, 128)] = mask * residual
        masked_p[rows, pl.ds(at + PAD, 128)] = mask * direction
        r_own[:, pl.ds(at, 128)] = residual[8:16]
        p_own[:, pl.ds(at, 128)] = direction[8:16]
        return carry

    lax.fori_loop(0, blocks, next_round, 0, unroll=8)
    wrap(masked_r, (8, 32), columns)
    wrap(masked_p, (8, 32), columns)

    for first, chain, length in ((masked_p, p_chain, STEPS), (masked_r, r_chain, STEPS - 1)):
        source = first
        for j in range(length):
            fold_top(source)
            rows = (16, 24) if j == length - 1 else (8, 32)
            operator(source, chain[j], quarter_mask, columns, SHIFTS[j], rows, (8, 32))
            source = chain[j]
    shared = gram_message(
        [own_of(p_own, 0)] + [own_of(p, PAD) for p in p_chain] + [own_of(r_own, 0)] + [own_of(r, PAD) for r in r_chain],
        columns,
    )
    message[1] = shared
    received[1, tile] = shared
    reduce_over_tiles(1)

    def part_one(block, carry):
        at = pl.multiple_of(block * 128, 128)
        held = [field[OWN, pl.ds(at, 128)]] + [v[OWN, pl.ds(at + PAD, 128)] for v in v_chain[: STEPS - 1]]
        result[:, pl.ds(at, 128)] = sum(coef[j : j + 1, :] * held[j] for j in range(STEPS))
        return carry

    lax.fori_loop(0, blocks, part_one, 0, unroll=8)
    x_col, r_col, d_col = coefficient_cg(sum_over_tiles(1), (STEPS + 1, STEPS), diffusivity, STEPS, True)
    coef[0:16, :] = x_col

    pieces = 4
    per_piece = blocks // pieces

    def finish(piece, carry):
        def part_two(block, carry):
            at = pl.multiple_of((piece * per_piece + block) * 128, 128)
            held = [p_own[:, pl.ds(at, 128)]] + [p[OWN, pl.ds(at + PAD, 128)] for p in p_chain[: STEPS - 1]]
            value = sum(coef[j : j + 1, :] * held[j] for j in range(STEPS))
            held = [r_own[:, pl.ds(at, 128)]] + [r[OWN, pl.ds(at + PAD, 128)] for r in r_chain[: STEPS - 2]]
            value += sum(coef[STEPS + 1 + j : STEPS + 2 + j, :] * held[j] for j in range(STEPS - 1))
            result[:, pl.ds(at, 128)] += value
            return carry

        lax.fori_loop(0, per_piece, part_two, 0, unroll=True)
        here = pl.ds(pl.multiple_of(piece * per_piece * 128, 128), per_piece * 128)
        pltpu.make_async_remote_copy(
            src_ref=result.at[:, here],
            dst_ref=other_out.at[:, here],
            send_sem=last_send,
            recv_sem=last_recv,
            device_id={"var": 1 - var},
            device_id_type=MESH,
        ).start()
        return carry

    lax.fori_loop(0, pieces, finish, 0)
    keep = pltpu.make_async_copy(result, solved_out, last_local)
    keep.start()

    def sent(buffer, sem):
        pltpu.make_async_copy(buffer, buffer, sem).wait()

    sent(rhs.at[0 : levels - 1], there_send)
    sent(rhs.at[0 : levels - 1], back_send)
    halo_wait(quarter_mask, mask_send, False)
    halo_wait(field, halo_send, False)
    for index in range(2):
        sent(received.at[index, 0 : tiles - 1], sum_send.at[index])
    keep.wait()
    sent(result, last_send)
    pltpu.make_async_copy(other_out, other_out, last_recv).wait()


def per_device(
    background, norm_factor, v_diffusivity, h_diffusivity, sea_mask, fold_order, coupling
):
    rows, columns = background.shape[2:]
    levels, tiles = lax.axis_size("lev"), lax.axis_size("tile")
    part = columns // levels
    f32 = jnp.float32
    strip = jax.ShapeDtypeStruct((rows, columns), f32)
    vmem = pltpu.VMEM
    tall = vmem((40, columns), f32)
    padded = vmem((40, columns + 2 * PAD), f32)
    blocks = columns // 128
    dma = pltpu.SemaphoreType.DMA
    solved, other = pl.pallas_call(
        kernel,
        out_shape=(strip, strip),
        in_specs=[pl.BlockSpec(memory_space=pl.ANY)] * 3
        + [pl.BlockSpec(memory_space=pltpu.SMEM)]
        + [pl.BlockSpec(memory_space=pl.ANY)] * 2,
        out_specs=(pl.BlockSpec(memory_space=pl.ANY),) * 2,
        scratch_shapes=[
            vmem((rows, columns), f32),
            vmem((rows, columns), f32),
            vmem((levels, rows, part), f32),
            vmem((rows, columns), jnp.int32),
            vmem((1, columns), jnp.int32),
            vmem((rows, columns), f32),
            vmem((levels, rows, part), f32),
            vmem((levels, rows, part), f32),
            vmem((levels, rows, part), f32),
            vmem((levels, rows, part), f32),
            vmem((levels, rows, part), f32),
            tall,
            tall,
            [padded] * STEPS,
            [padded] * STEPS,
            [padded] * (STEPS - 1),
            padded,
            padded,
            vmem((rows, columns), f32),
            vmem((rows, columns), f32),
            vmem((blocks, 128), jnp.int32),
            vmem((blocks, 128), jnp.int32),
            vmem((blocks, 128), f32),
            vmem((2, 1, 128), f32),
            vmem((2, tiles, 1, 128), f32),
            vmem((rows, columns), f32),
            vmem((48, 128), f32),
            dma((5,)),
            dma,
            dma,
            dma,
            dma((levels,)),
            dma((4,)),
            dma((4,)),
            dma((4,)),
            dma((4,)),
            dma((2,)),
            dma((2,)),
            dma,
            dma,
            dma,
        ],
        compiler_params=pltpu.CompilerParams(
            collective_id=0, has_side_effects=True, vmem_limit_bytes=40 * 2**20
        ),
    )(
        background.reshape(rows, columns),
        norm_factor.reshape(rows, columns),
        v_diffusivity.reshape(levels, rows, part),
        h_diffusivity,
        sea_mask.reshape(rows, columns),
        fold_order.reshape(1, columns),
    )
    return (solved + coupling[0, 0] * other)[None, None]


def solution(mesh):
    placed = (
        P("var", "lev", "tile", None),
        P("var", "lev", "tile", None),
        P("var", None, "tile", "lev"),
        P("var", "lev"),
        P("lev", "tile", None),
        P(),
        P("var", "lev", "tile", None),
    )
    return jax.shard_map(
        per_device,
        mesh=mesh,
        in_specs=placed,
        out_specs=P("var", "lev", "tile", None),
        check_vma=False,
    )
```

time: 1820 us -> 67.1 us (0.04)
  the two profiles are of different devices: /device:TPU:72 before, /device:TPU:8 now
where the time goes in v1:
time: 67.1 us; the launch traced here: 66.8 us
  Pallas kernels  61.2 us (91%)
  local copies, waits for them, and re-layouts  4.33 us (6%)
  other arithmetic  0.68 us (1%)
  between operations  0.68 us (1%)
    pallas_call x1, Pallas kernels, per_device(): pl.pallas_call(kernel, out_shape=(strip, strip), in_specs=[pl.BlockSpec(m...  61.2 us
    unnamed x12, local copies, waits for them, and re-layouts  4.33 us

profile of v1, /device:TPU:8, one launch (start us, length us, event | category | flops | bytes accessed | tf_op | source)
XLA Modules:
  0.0 66.8 jit_solution(1088763311358272520)
XLA Ops:
  0.7 0.0 copy-start
  0.7 0.9 %copy-done = f32[1,1,8,4096]{3,2,1,0:T(8,128)S(1)} copy-done((f32[1,1,8,4096]{3,2,1,0:T(8,128)S(1)}, f32[1,1,8,4096]{3,2,1,0:T(8,128)}, u32[]{:S(2)}) %copy-start) | copy-done | bytes 131096
  1.6 0.0 copy-start.1
  1.6 0.9 %copy-done.1 = f32[1,1,8,4096]{3,2,1,0:T(8,128)S(1)} copy-done((f32[1,1,8,4096]{3,2,1,0:T(8,128)S(1)}, f32[1,1,8,4096]{3,2,1,0:T(8,128)}, u32[]{:S(2)}) %copy-start.1) | copy-done | bytes 131096
  2.5 0.0 copy-start.2
  2.5 0.9 %copy-done.2 = f32[1,8,8,512]{3,2,1,0:T(8,128)S(1)} copy-done((f32[1,8,8,512]{3,2,1,0:T(8,128)S(1)}, f32[1,8,8,512]{3,2,1,0:T(8,128)}, u32[]{:S(2)}) %copy-start.2) | copy-done | bytes 131096
  3.4 0.0 copy-start.3
  3.4 0.9 %copy-done.3 = s32[1,8,4096]{2,1,0:T(8,128)S(1)} copy-done((s32[1,8,4096]{2,1,0:T(8,128)S(1)}, s32[1,8,4096]{2,1,0:T(8,128)}, u32[]{:S(2)}) %copy-start.3) | copy-done | bytes 131096
  4.3 0.0 copy-start.4
  4.3 0.7 %copy-done.4 = s32[4096]{0:T(1024)S(1)} copy-done((s32[4096]{0:T(1024)S(1)}, s32[4096]{0:T(1024)}, u32[]{:S(2)}) %copy-start.4) | copy-done | bytes 16408
  5.0 0.0 copy-start.5
  5.0 61.2 %shard_map.73 = (f32[8,4096]{1,0:T(8,128)S(1)}, f32[8,4096]{1,0:T(8,128)S(1)}) custom-call(f32[8,4096]{1,0:T(8,128)S(1)} %bitcast.13, f32[8,4096]{1,0:T(8,128)S(1)} %bitcast.14, f32[8,8,512]{2,1,0:T(8,128)S(1)} %bitcast.15, f32[1,1]{1,0:T(1,128)S(6)} %copy.8.h_diffusivity, s32[8,4096]{1,0:T(8,128)S(1)} %bitcast.16, s32[1,4096]{1,0:T(1,128)S(1)} %bitcast.17), custom_call_target="tpu_custom_call" | custom-call | tf_op jit(solution)/shard_map/pallas_call | solution.py:467
  66.2 0.0 copy-done.5
  66.2 0.7 %fusion.1 = f32[1,1,8,4096]{3,2,1,0:T(8,128)} fusion(f32[8,4096]{1,0:T(8,128)S(1)} %get-tuple-element.7, f32[8,4096]{1,0:T(8,128)S(1)} %get-tuple-element.8, f32[1,1,8,4096]{3,2,1,0:T(8,128)S(1)} %copy-done.5), kind=kLoop, calls=%fused_computation.2 | loop fusion | flops 65536 | bytes 524288 | tf_op jit(solution)/shard_map/broadcast_in_dim | solution.py:528
Async XLA Ops:
  0.7 0.9 %copy-start = (f32[1,1,8,4096]{3,2,1,0:T(8,128)S(1)}, f32[1,1,8,4096]{3,2,1,0:T(8,128)}, u32[]{:S(2)}) copy-start(f32[1,1,8,4096]{3,2,1,0:T(8,128)} %param.7) | copy-start | bytes 393220
  1.6 0.9 %copy-start.1 = (f32[1,1,8,4096]{3,2,1,0:T(8,128)S(1)}, f32[1,1,8,4096]{3,2,1,0:T(8,128)}, u32[]{:S(2)}) copy-start(f32[1,1,8,4096]{3,2,1,0:T(8,128)} %param.8) | copy-start | bytes 393220
  2.5 0.9 %copy-start.2 = (f32[1,8,8,512]{3,2,1,0:T(8,128)S(1)}, f32[1,8,8,512]{3,2,1,0:T(8,128)}, u32[]{:S(2)}) copy-start(f32[1,8,8,512]{3,2,1,0:T(8,128)} %param.9) | copy-start | bytes 393220
  3.4 0.9 %copy-start.3 = (s32[1,8,4096]{2,1,0:T(8,128)S(1)}, s32[1,8,4096]{2,1,0:T(8,128)}, u32[]{:S(2)}) copy-start(s32[1,8,4096]{2,1,0:T(8,128)} %param.11) | copy-start | bytes 393220
  4.3 0.7 %copy-start.4 = (s32[4096]{0:T(1024)S(1)}, s32[4096]{0:T(1024)}, u32[]{:S(2)}) copy-start(s32[4096]{0:T(1024)} %param.12) | copy-start | bytes 49156
  5.0 61.2 %copy-start.5 = (f32[1,1,8,4096]{3,2,1,0:T(8,128)S(1)}, f32[1,1,8,4096]{3,2,1,0:T(8,128)}, u32[]{:S(2)}) copy-start(f32[1,1,8,4096]{3,2,1,0:T(8,128)} %param.13) | copy-start | bytes 393220

commit v2 on v1

--- a/solution.py
+++ b/solution.py
@@ -9,7 +9,7 @@
 
 MESH = pl.DeviceIdType.MESH
 STEPS = 5
-SHIFTS = (0.0, 6.0, 3.0, 7.0, 1.5)
+SHIFTS = (0.0, 5.0, 2.0, 7.0, 0.5)
 ROWS = 8
 PAD = 128
 OWN = slice(16, 24)
@@ -163,8 +163,8 @@
         pl.semaphore_signal(barrier, inc=1, device_id={"tile": lax.rem(tile + d, tiles)}, device_id_type=MESH)
         return carry
 
-    lax.fori_loop(1, levels, greet_level, 0)
-    lax.fori_loop(1, tiles, greet_tile, 0)
+    lax.fori_loop(1, levels, greet_level, 0, unroll=True)
+    lax.fori_loop(1, tiles, greet_tile, 0, unroll=True)
     pl.semaphore_signal(barrier, inc=1, device_id={"var": 1 - var}, device_id_type=MESH)
     loads[0].wait()
     loads[1].wait()
@@ -185,7 +185,7 @@
         ).start()
         return carry
 
-    lax.fori_loop(1, levels, send_there, 0)
+    lax.fori_loop(1, levels, send_there, 0, unroll=True)
     rhs[lev] = scaled[:, pl.ds(pl.multiple_of(lev * part, part), part)]
 
     sides = ((16, 24, 8, 1), (16, 24, 24, -1), (22, 24, 6, 2), (16, 18, 32, -2))
@@ -271,7 +271,7 @@
         ).start()
         return carry
 
-    lax.fori_loop(1, levels, send_back, 0)
+    lax.fori_loop(1, levels, send_back, 0, unroll=True)
     field[OWN, pl.ds(my_columns, part)] = solved[lev]
     halo_copies(field, halo_send, halo_recv, my_columns, part)
 
@@ -349,7 +349,7 @@
             ).start()
             return carry
 
-        lax.fori_loop(1, tiles, send, 0)
+        lax.fori_loop(1, tiles, send, 0, unroll=True)
 
     def sum_over_tiles(index):
         others = received.at[index, 0 : tiles - 1]
@@ -464,6 +464,7 @@
     padded = vmem((40, columns + 2 * PAD), f32)
     blocks = columns // 128
     dma = pltpu.SemaphoreType.DMA
+    in_hbm = functools.partial(pltpu.with_memory_space_constraint, memory_space=pltpu.HBM)
     solved, other = pl.pallas_call(
         kernel,
         out_shape=(strip, strip),
@@ -518,12 +519,12 @@
             collective_id=0, has_side_effects=True, vmem_limit_bytes=40 * 2**20
         ),
     )(
-        background.reshape(rows, columns),
-        norm_factor.reshape(rows, columns),
-        v_diffusivity.reshape(levels, rows, part),
+        in_hbm(background.reshape(rows, columns)),
+        in_hbm(norm_factor.reshape(rows, columns)),
+        in_hbm(v_diffusivity.reshape(levels, rows, part)),
         h_diffusivity,
-        sea_mask.reshape(rows, columns),
-        fold_order.reshape(1, columns),
+        in_hbm(sea_mask.reshape(rows, columns)),
+        in_hbm(fold_order.reshape(1, columns)),
     )
     return (solved + coupling[0, 0] * other)[None, None]
 

time: 67.1 us -> 62 us (0.924)
  local copies, waits for them, and re-layouts: 4.33 us -> 0.01 us
  Pallas kernels: 61.2 us -> 60.5 us
    unnamed x12 -> x2, local copies, waits for them, and re-layouts: 4.33 us -> 0.01 us
    pallas_call x1, Pallas kernels: 61.2 us -> 60.5 us  [per_device(): pl.pallas_call(kernel, out_shape=(strip, strip), in_specs=[pl.BlockSpec(m...]
where the time goes in v2:
time: 62 us; the launch traced here: 61.8 us
  Pallas kernels  60.5 us (98%)
  other arithmetic  0.68 us (1%)
  between operations  0.68 us (1%)
    pallas_call x1, Pallas kernels, per_device(): pl.pallas_call(kernel, out_shape=(strip, strip), in_specs=[pl.BlockSpec(m...  60.5 us

profile of v2, /device:TPU:8, one launch (start us, length us, event | category | flops | bytes accessed | tf_op | source)
XLA Modules:
  0.0 61.8 jit_solution(9233190140100518068)
XLA Ops:
  0.7 0.0 copy-start
  0.7 60.5 %shard_map.73 = (f32[8,4096]{1,0:T(8,128)S(1)}, f32[8,4096]{1,0:T(8,128)S(1)}) custom-call(f32[8,4096]{1,0:T(8,128)} %bitcast.13, f32[8,4096]{1,0:T(8,128)} %bitcast.14, f32[8,8,512]{2,1,0:T(8,128)} %bitcast.15, f32[1,1]{1,0:T(1,128)S(6)} %copy.8.h_diffusivity, s32[8,4096]{1,0:T(8,128)} %bitcast.16, s32[1,4096]{1,0:T(1,128)} %bitcast.17), custom_call_target="tpu_custom_call" | custom-call | tf_op jit(solution)/shard_map/pallas_call | solution.py:468
  61.1 0.0 copy-done
  61.2 0.7 %fusion.1 = f32[1,1,8,4096]{3,2,1,0:T(8,128)} fusion(f32[8,4096]{1,0:T(8,128)S(1)} %get-tuple-element.7, f32[8,4096]{1,0:T(8,128)S(1)} %get-tuple-element.8, f32[1,1,8,4096]{3,2,1,0:T(8,128)S(1)} %copy-done), kind=kLoop, calls=%fused_computation.2 | loop fusion | flops 65536 | bytes 524288 | tf_op jit(solution)/shard_map/broadcast_in_dim | solution.py:529
Async XLA Ops:
  0.7 60.5 %copy-start = (f32[1,1,8,4096]{3,2,1,0:T(8,128)S(1)}, f32[1,1,8,4096]{3,2,1,0:T(8,128)}, u32[]{:S(2)}) copy-start(f32[1,1,8,4096]{3,2,1,0:T(8,128)} %param.13) | copy-start | bytes 393220

commit v3 on v2

--- a/solution.py
+++ b/solution.py
@@ -130,9 +130,9 @@
     solved_out, other_out,
     bg, nf, vd, mask_in, fold_in, scaled, rhs, solved, inverse, below, upper,
     field, quarter_mask, v_chain, p_chain, r_chain, masked_p, masked_r, p_own, r_own,
-    partner_row, partner_lane, folded, message, received, result, coef,
+    partner_row, partner_lane, folded, message, received, result, halfway, coef,
     load_sem, there_send, there_recv, back_send, back_recv,
-    halo_send, halo_recv, mask_send, mask_recv, sum_send, sum_recv, last_send, last_recv, last_local,
+    halo_send, halo_recv, mask_send, mask_recv, sum_send, sum_recv, last_send, half_recv, last_recv, last_local,
 ):
     tile, lev, var = (lax.axis_index(a) for a in ("tile", "lev", "var"))
     tiles, levels = lax.axis_size("tile"), lax.axis_size("lev")
@@ -150,42 +150,46 @@
     ]
     for load in loads:
         load.start()
-    for buffer in (field, quarter_mask):
-        for low in (0, 8, 24, 32):
-            buffer[low : low + 8, :] = jnp.zeros((8, columns), f32)
     barrier = pltpu.get_barrier_semaphore()
-
-    def greet_level(d, carry):
-        pl.semaphore_signal(barrier, inc=1, device_id={"lev": lax.rem(lev + d, levels)}, device_id_type=MESH)
-        return carry
+    bits = (lax.rem(lev, 2), lax.rem(lev // 2, 2), lev // 4)
+
+    def peer_level(d):
+        return sum(
+            (1 - bit if d >> place & 1 else bit) * (1 << place) for place, bit in enumerate(bits)
+        )
+
+    peers = [peer_level(d) for d in range(levels)]
+    chip = 4 * var + lev // 2
+
+    def along(hops):
+        place = lax.rem(chip + hops + 8, 8)
+        return {"var": place // 4, "lev": 2 * lax.rem(place, 4) + bits[0]}
 
     def greet_tile(d, carry):
         pl.semaphore_signal(barrier, inc=1, device_id={"tile": lax.rem(tile + d, tiles)}, device_id_type=MESH)
         return carry
 
-    lax.fori_loop(1, levels, greet_level, 0, unroll=True)
+    for d in range(1, levels):
+        pl.semaphore_signal(barrier, inc=1, device_id={"lev": peers[d]}, device_id_type=MESH)
+    for hops in (2, -2):
+        pl.semaphore_signal(barrier, inc=1, device_id=along(hops), device_id_type=MESH)
     lax.fori_loop(1, tiles, greet_tile, 0, unroll=True)
-    pl.semaphore_signal(barrier, inc=1, device_id={"var": 1 - var}, device_id_type=MESH)
     loads[0].wait()
     loads[1].wait()
     scaled[...] = nf[...] * bg[...]
     loads[2].wait()
     quarter_mask[OWN, :] = 0.25 * mask_in[...].astype(f32)
-    pl.semaphore_wait(barrier, (levels - 1) + (tiles - 1) + 1)
-
-    def send_there(d, carry):
-        to = lax.rem(lev + d, levels)
+    pl.semaphore_wait(barrier, (levels - 1) + (tiles - 1) + 2)
+
+    for d in reversed(range(1, levels)):
         pltpu.make_async_remote_copy(
-            src_ref=scaled.at[:, pl.ds(pl.multiple_of(to * part, part), part)],
+            src_ref=scaled.at[:, pl.ds(pl.multiple_of(peers[d] * part, part), part)],
             dst_ref=rhs.at[lev],
             send_sem=there_send,
             recv_sem=there_recv,
-            device_id={"lev": to},
+            device_id={"lev": peers[d]},
             device_id_type=MESH,
         ).start()
-        return carry
-
-    lax.fori_loop(1, levels, send_there, 0, unroll=True)
     rhs[lev] = scaled[:, pl.ds(pl.multiple_of(lev * part, part), part)]
 
     sides = ((16, 24, 8, 1), (16, 24, 24, -1), (22, 24, 6, 2), (16, 18, 32, -2))
@@ -216,6 +220,13 @@
                 pltpu.make_async_copy(buffer.at[at, :], buffer.at[at, :], sem.at[side]).wait()
 
     halo_copies(quarter_mask, mask_send, mask_recv, 0, columns)
+    for side, (_, _, land, distance) in enumerate(sides):
+        low = land // 8 * 8
+
+        @pl.when(jnp.logical_not(reached(-distance)))
+        def _(low=low):
+            for buffer in (field, quarter_mask):
+                buffer[low : low + 8, :] = jnp.zeros((8, columns), f32)
 
     loads[3].wait()
     above = jnp.zeros((ROWS, part), f32)
@@ -259,30 +270,23 @@
 
     my_columns = pl.multiple_of(lev * part, part)
 
-    def send_back(d, carry):
-        to = lax.rem(lev + d, levels)
+    for d in reversed(range(1, levels)):
         pltpu.make_async_remote_copy(
-            src_ref=solved.at[to],
+            src_ref=solved.at[peers[d]],
             dst_ref=field.at[OWN, pl.ds(my_columns, part)],
             send_sem=back_send,
             recv_sem=back_recv.at[d],
-            device_id={"lev": to},
+            device_id={"lev": peers[d]},
             device_id_type=MESH,
         ).start()
-        return carry
-
-    lax.fori_loop(1, levels, send_back, 0, unroll=True)
     field[OWN, pl.ds(my_columns, part)] = solved[lev]
     halo_copies(field, halo_send, halo_recv, my_columns, part)
 
-    def pass_on(d, carry):
-        at = pl.multiple_of(lax.rem(lev + levels - d, levels) * part, part)
+    for d in range(1, levels):
+        at = pl.multiple_of(peers[d] * part, part)
         here = field.at[OWN, pl.ds(at, part)]
         pltpu.make_async_copy(here, here, back_recv.at[d]).wait()
         halo_copies(field, halo_send, halo_recv, at, part)
-        return carry
-
-    lax.fori_loop(1, levels, pass_on, 0)
 
     def fold(buffer, last_row):
         sums = tuple(jnp.zeros((8, 128), f32) for _ in range(blocks // 8))
@@ -408,11 +412,25 @@
     x_col, r_col, d_col = coefficient_cg(sum_over_tiles(1), (STEPS + 1, STEPS), diffusivity, STEPS, True)
     coef[0:16, :] = x_col
 
-    pieces = 4
-    per_piece = blocks // pieces
-
-    def finish(piece, carry):
-        def part_two(block, carry):
+    pieces = 8
+    width = columns // pieces
+    per_piece = width // 128
+    ways = (2, -2)
+
+    def leg(source, target, piece, index):
+        here = pl.ds(pl.multiple_of(piece * width, width), width)
+        return pltpu.make_async_remote_copy(
+            src_ref=source.at[:, here],
+            dst_ref=target.at[:, here],
+            send_sem=last_send.at[index],
+            recv_sem=half_recv.at[piece] if index == 0 else last_recv,
+            device_id=along(ways[piece % 2]),
+            device_id_type=MESH,
+        )
+
+    for piece in range(pieces):
+
+        def part_two(block, carry, piece=piece):
             at = pl.multiple_of((piece * per_piece + block) * 128, 128)
             held = [p_own[:, pl.ds(at, 128)]] + [p[OWN, pl.ds(at + PAD, 128)] for p in p_chain[: STEPS - 1]]
             value = sum(coef[j : j + 1, :] * held[j] for j in range(STEPS))
@@ -422,18 +440,11 @@
             return carry
 
         lax.fori_loop(0, per_piece, part_two, 0, unroll=True)
-        here = pl.ds(pl.multiple_of(piece * per_piece * 128, 128), per_piece * 128)
-        pltpu.make_async_remote_copy(
-            src_ref=result.at[:, here],
-            dst_ref=other_out.at[:, here],
-            send_sem=last_send,
-            recv_sem=last_recv,
-            device_id={"var": 1 - var},
-            device_id_type=MESH,
-        ).start()
-        return carry
-
-    lax.fori_loop(0, pieces, finish, 0)
+        leg(result, halfway, piece, 0).start()
+    for piece in range(pieces):
+        arrived = halfway.at[:, piece * width : (piece + 1) * width]
+        pltpu.make_async_copy(arrived, arrived, half_recv.at[piece]).wait()
+        leg(halfway, other_out, piece, 1).start()
     keep = pltpu.make_async_copy(result, solved_out, last_local)
     keep.start()
 
@@ -447,7 +458,8 @@
     for index in range(2):
         sent(received.at[index, 0 : tiles - 1], sum_send.at[index])
     keep.wait()
-    sent(result, last_send)
+    sent(result, last_send.at[0])
+    sent(result, last_send.at[1])
     pltpu.make_async_copy(other_out, other_out, last_recv).wait()
 
 
@@ -499,6 +511,7 @@
             vmem((2, 1, 128), f32),
             vmem((2, tiles, 1, 128), f32),
             vmem((rows, columns), f32),
+            vmem((rows, columns), f32),
             vmem((48, 128), f32),
             dma((5,)),
             dma,
@@ -511,7 +524,8 @@
             dma((4,)),
             dma((2,)),
             dma((2,)),
-            dma,
+            dma((2,)),
+            dma((8,)),
             dma,
             dma,
         ],

time: 62 us -> 61.7 us (level)
  no operation moved by 1% of the time
where the time goes in v3:
time: 61.7 us; the launch traced here: 61.6 us
  Pallas kernels  60.2 us (98%)
  other arithmetic  0.68 us (1%)
  between operations  0.68 us (1%)
    pallas_call x1, Pallas kernels, per_device(): pl.pallas_call(kernel, out_shape=(strip, strip), in_specs=[pl.BlockSpec(m...  60.2 us

profile of v3, /device:TPU:8, one launch (start us, length us, event | category | flops | bytes accessed | tf_op | source)
XLA Modules:
  0.0 61.6 jit_solution(5734512635499403495)
XLA Ops:
  0.7 0.0 copy-start
  0.7 60.2 %shard_map.73 = (f32[8,4096]{1,0:T(8,128)S(1)}, f32[8,4096]{1,0:T(8,128)S(1)}) custom-call(f32[8,4096]{1,0:T(8,128)} %bitcast.13, f32[8,4096]{1,0:T(8,128)} %bitcast.14, f32[8,8,512]{2,1,0:T(8,128)} %bitcast.15, f32[1,1]{1,0:T(1,128)S(6)} %copy.8.h_diffusivity, s32[8,4096]{1,0:T(8,128)} %bitcast.16, s32[1,4096]{1,0:T(1,128)} %bitcast.17), custom_call_target="tpu_custom_call" | custom-call | tf_op jit(solution)/shard_map/pallas_call | solution.py:480
  60.9 0.0 copy-done
  60.9 0.7 %fusion.1 = f32[1,1,8,4096]{3,2,1,0:T(8,128)} fusion(f32[8,4096]{1,0:T(8,128)S(1)} %get-tuple-element.7, f32[8,4096]{1,0:T(8,128)S(1)} %get-tuple-element.8, f32[1,1,8,4096]{3,2,1,0:T(8,128)S(1)} %copy-done), kind=kLoop, calls=%fused_computation.2 | loop fusion | flops 65536 | bytes 524288 | tf_op jit(solution)/shard_map/broadcast_in_dim | solution.py:543
Async XLA Ops:
  0.7 60.3 %copy-start = (f32[1,1,8,4096]{3,2,1,0:T(8,128)S(1)}, f32[1,1,8,4096]{3,2,1,0:T(8,128)}, u32[]{:S(2)}) copy-start(f32[1,1,8,4096]{3,2,1,0:T(8,128)} %param.13) | copy-start | bytes 393220

commit v4 on v3

v4 whole, which is shorter than its diff:
```python
import functools

import jax
import jax.numpy as jnp
from jax import lax
from jax.experimental import pallas as pl
from jax.experimental.pallas import tpu as pltpu
from jax.sharding import PartitionSpec as P

MESH = pl.DeviceIdType.MESH
ROUNDS = (5, 5)
SHIFTS = (0.0, 5.0, 2.0, 7.0, 0.5)
ROWS = 8
PAD = 128
OWN = slice(8, 16)


def tree_sum(terms):
    terms = list(terms)
    while len(terms) > 1:
        terms = [sum(terms[i : i + 2]) for i in range(0, len(terms), 2)]
    return terms[0]


def pairs_of(count):
    return [(i, j) for i in range(count) for j in range(i, count)]


def gram_message(vectors, columns):
    pairs = pairs_of(len(vectors))
    lane = lax.broadcasted_iota(jnp.int32, (8, 128), 1)
    message = jnp.zeros((8, 128), jnp.float32)
    for at in range(0, len(pairs), 28):
        group = pairs[at : at + 28]
        used = sorted({i for pair in group for i in pair})

        def body(block, sums, group=group, used=used):
            held = {i: vectors[i](block) for i in used}
            return tuple(total + held[i] * held[j] for total, (i, j) in zip(sums, group))

        zeros = tuple(jnp.zeros((8, 128), jnp.float32) for _ in group)
        sums = lax.fori_loop(0, columns // 128, body, zeros, unroll=8)
        for place, total in enumerate(sums):
            message = jnp.where(lane == at + place, jnp.sum(total, axis=1, keepdims=True), message)
    return jnp.sum(message, axis=0, keepdims=True)


def coefficient_cg(totals, chains, diffusivity, steps, last):
    count = sum(chains)
    first = count - chains[-1]
    totals = jnp.broadcast_to(totals, (8, 128))
    gram = {}
    for place, (i, j) in enumerate(pairs_of(count)):
        gram[i, j] = gram[j, i] = jnp.broadcast_to(totals[:, place : place + 1], (8, 128))
    same, start = {}, 0
    for length in chains:
        for j in range(length - 1):
            same[start + j] = 1.0 + diffusivity * SHIFTS[j]
        start += length
    up = 4.0 * diffusivity

    def image_of(d):
        parts = {}
        for j, value in d.items():
            parts.setdefault(j, []).append(same[j] * value)
            parts.setdefault(j + 1, []).append(up * value)
        return {j: sum(terms) for j, terms in sorted(parts.items())}

    def product(u, v):
        return tree_sum(u[i] * tree_sum(gram[i, j] * v[j] for j in v) for i in u)

    def add(u, factor, v):
        return {j: (u[j] if j in u else 0.0) + (factor * v[j] if j in v else 0.0) for j in sorted({*u, *v})}

    d, r, x = {0: 1.0}, {first: 1.0}, {}
    norm_now = gram[first, first]
    for step in range(steps):
        image = image_of(d)
        energy = product(d, image)
        size = jnp.where(energy > 0, jnp.minimum(norm_now / energy, 1.0), 0.0)
        x = add(x, size, d)
        if last and step == steps - 1:
            break
        r = add(r, -size, image)
        norm_next = jnp.maximum(product(r, r), 0.0)
        d = add(r, jnp.where(norm_now > 0, norm_next / norm_now, 0.0), d)
        norm_now = norm_next
    return x, r, d


def packed(tall):
    upper_half = lax.broadcasted_iota(jnp.int32, (8, 128), 0) < 4
    return jnp.concatenate([tall[8:16], jnp.where(upper_half, tall[16:24], tall[0:8])], axis=0)


def operator(source, target, quarter_mask, columns, shift, rows, loaded, pack=False, group=8):
    lane = lax.broadcasted_iota(jnp.int32, (rows, 128), 1)
    cut = packed if pack else lambda value: value[0:rows]

    def body(chunk, carry):
        at = pl.multiple_of(chunk * (group * 128), 128)
        held, ahead, behind = {}, {}, {}
        for k in range(group + 2):
            held[k] = source[0:loaded, pl.ds(at + 128 * k, 128)]
            ahead[k] = pltpu.roll(cut(held[k]), 127, 1)
            behind[k] = pltpu.roll(cut(held[k]), 1, 1)
            if k < 2:
                continue
            here = held[k - 1]
            east = jnp.where(lane == 127, ahead[k], ahead[k - 1])
            west = jnp.where(lane == 0, behind[k - 2], behind[k - 1])
            north = cut(pltpu.roll(here, loaded - 1, 0))
            south = cut(pltpu.roll(here, 1, 0))
            here = cut(here)
            value = 4.0 * here - ((north + south) + (east + west))
            value = quarter_mask[0:rows, pl.ds(at + 128 * (k - 2), 128)] * value
            if shift:
                value = value - (0.25 * shift) * here
            target[0:rows, pl.ds(at + 128 * (k - 1), 128)] = value
        return carry

    lax.fori_loop(0, columns // (group * 128), body, 0, unroll=True)
    wrap(target, rows, columns)


def wrap(target, rows, columns):
    target[0:rows, 0:PAD] = target[0:rows, columns : columns + PAD]
    target[0:rows, columns + PAD : columns + 2 * PAD] = target[0:rows, PAD : 2 * PAD]


def kernel(
    background, norm_factor, v_diffusivity, h_diffusivity, sea_mask, fold_order,
    solved_out, other_out,
    bg, nf, vd, mask_in, fold_in, scaled, rhs, solved, inverse, below, upper,
    field, quarter_mask, packed_mask, masked, v_chain, p_chain, r_chain, masked_p, masked_r, p_own, r_own,
    partner_row, partner_lane, folded, message, received, result,
    load_sem, there_send, there_recv, back_send, back_recv,
    halo_send, halo_recv, mask_send, mask_recv, sum_send, sum_recv, last_send, last_recv, last_local,
):
    tile, lev, var = (lax.axis_index(a) for a in ("tile", "lev", "var"))
    tiles, levels = lax.axis_size("tile"), lax.axis_size("lev")
    columns = bg.shape[1]
    part = columns // levels
    top = tiles - 1
    blocks = columns // 128
    f32 = jnp.float32

    loads = [
        pltpu.make_async_copy(source, target, load_sem.at[i])
        for i, (source, target) in enumerate(
            ((background, bg), (norm_factor, nf), (sea_mask, mask_in), (v_diffusivity, vd), (fold_order, fold_in))
        )
    ]
    for load in loads:
        load.start()
    barrier = pltpu.get_barrier_semaphore()
    bits = (lax.rem(lev, 2), lax.rem(lev // 2, 2), lev // 4)

    def peer_level(d):
        return sum(
            (1 - bit if d >> place & 1 else bit) * (1 << place) for place, bit in enumerate(bits)
        )

    peers = [peer_level(d) for d in range(levels)]

    def greet_tile(d, carry):
        pl.semaphore_signal(barrier, inc=1, device_id={"tile": lax.rem(tile + d, tiles)}, device_id_type=MESH)
        return carry

    for d in range(1, levels):
        pl.semaphore_signal(barrier, inc=1, device_id={"lev": peers[d]}, device_id_type=MESH)
    pl.semaphore_signal(barrier, inc=1, device_id={"var": 1 - var}, device_id_type=MESH)
    lax.fori_loop(1, tiles, greet_tile, 0, unroll=True)
    loads[0].wait()
    loads[1].wait()
    scaled[...] = nf[...] * bg[...]
    loads[2].wait()
    quarter_mask[OWN, :] = 0.25 * mask_in[...].astype(f32)
    pl.semaphore_wait(barrier, (levels - 1) + (tiles - 1) + 1)

    for d in reversed(range(1, levels)):
        pltpu.make_async_remote_copy(
            src_ref=scaled.at[:, pl.ds(pl.multiple_of(peers[d] * part, part), part)],
            dst_ref=rhs.at[lev],
            send_sem=there_send,
            recv_sem=there_recv,
            device_id={"lev": peers[d]},
            device_id_type=MESH,
        ).start()
    rhs[lev] = scaled[:, pl.ds(pl.multiple_of(lev * part, part), part)]

    sides = ((8, 16, 0, 1), (8, 16, 16, -1), (14, 16, 30, 2), (8, 10, 24, -2))

    def reached(distance):
        return tile + distance <= top if distance > 0 else tile + distance >= 0

    def halo_copies(buffer, send, recv, at, width):
        for side, (low, high, land, distance) in enumerate(sides):

            @pl.when(reached(distance))
            def _(side=side, low=low, high=high, land=land, distance=distance):
                pltpu.make_async_remote_copy(
                    src_ref=buffer.at[low:high, pl.ds(at, width)],
                    dst_ref=buffer.at[land : land + high - low, pl.ds(at, width)],
                    send_sem=send.at[side],
                    recv_sem=recv.at[side],
                    device_id={"tile": tile + distance},
                    device_id_type=MESH,
                ).start()

    def halo_wait(buffer, sem, receive):
        for side, (low, high, land, distance) in enumerate(sides):

            @pl.when(reached(-distance if receive else distance))
            def _(side=side, low=low, high=high, land=land):
                at = slice(land, land + high - low) if receive else slice(low, high)
                pltpu.make_async_copy(buffer.at[at, :], buffer.at[at, :], sem.at[side]).wait()

    halo_copies(quarter_mask, mask_send, mask_recv, 0, columns)
    for low, high, land, distance in sides:

        @pl.when(jnp.logical_not(reached(-distance)))
        def _(land=land, rows=high - low):
            for buffer in (field, quarter_mask):
                buffer[land : land + rows, :] = jnp.zeros((rows, columns), f32)

    loads[3].wait()
    above = jnp.zeros((ROWS, part), f32)
    upper_now = above
    for level in range(levels):
        coefficient = vd[level]
        inv = 1.0 / (1.0 + above + coefficient + above * upper_now)
        inverse[level] = inv
        below[level] = above * inv
        upper_now = -coefficient * inv
        upper[level] = upper_now
        above = coefficient

    loads[4].wait()

    @pl.when(tile >= top - 1)
    def _():
        order = fold_in[...]
        lane = lax.broadcasted_iota(jnp.int32, (1, columns), 1)
        mate = jnp.where(lane % 2 == 0, pltpu.roll(order, columns - 1, 1), pltpu.roll(order, 1, 1))
        row_hot = lax.broadcasted_iota(jnp.int32, (blocks, columns), 0) == order // 128
        lane_hot = lax.broadcasted_iota(jnp.int32, (128, columns), 0) == order % 128
        high = jnp.where(row_hot, (mate // 64).astype(f32), 0.0)
        low = jnp.where(row_hot, (mate % 64).astype(f32), 0.0)
        left = jnp.concatenate([high, low], axis=0).astype(jnp.bfloat16)
        right = jnp.where(lane_hot, 1.0, 0.0).astype(jnp.bfloat16)
        found = lax.dot_general(left, right, (((1,), (1,)), ((), ())), preferred_element_type=f32)
        partner = 64 * found[:blocks].astype(jnp.int32) + found[blocks:].astype(jnp.int32)
        partner_row[...] = partner // 128
        partner_lane[...] = partner % 128

    pltpu.make_async_copy(rhs.at[0 : levels - 1], rhs.at[0 : levels - 1], there_recv).wait()
    reduced = jnp.zeros((ROWS, part), f32)
    for level in range(levels):
        reduced = rhs[level] * inverse[level] + below[level] * reduced
        solved[level] = reduced
    value = jnp.zeros((ROWS, part), f32)
    for level in reversed(range(levels)):
        value = solved[level] - upper[level] * value
        solved[level] = value

    my_columns = pl.multiple_of(lev * part, part)

    for d in reversed(range(1, levels)):
        pltpu.make_async_remote_copy(
            src_ref=solved.at[peers[d]],
            dst_ref=field.at[OWN, pl.ds(my_columns, part)],
            send_sem=back_send,
            recv_sem=back_recv.at[d],
            device_id={"lev": peers[d]},
            device_id_type=MESH,
        ).start()
    field[OWN, pl.ds(my_columns, part)] = solved[lev]
    halo_copies(field, halo_send, halo_recv, my_columns, part)

    for d in range(1, levels):
        at = pl.multiple_of(peers[d] * part, part)
        here = field.at[OWN, pl.ds(at, part)]
        pltpu.make_async_copy(here, here, back_recv.at[d]).wait()
        halo_copies(field, halo_send, halo_recv, at, part)

    def fold(buffer, last_row):
        sums = tuple(jnp.zeros((8, 128), f32) for _ in range(blocks // 8))

        def pick(block, sums):
            at = pl.multiple_of(PAD + block * 128, 128)
            line = jnp.broadcast_to(buffer[last_row : last_row + 1, pl.ds(at, 128)], (8, 128))
            chosen = []
            for q, now in enumerate(sums):
                rows = slice(8 * q, 8 * q + 8)
                moved = jnp.take_along_axis(line, partner_lane[rows, :], axis=1)
                chosen.append(jnp.where(partner_row[rows, :] == block, moved, now))
            return tuple(chosen)

        sums = lax.fori_loop(0, blocks, pick, sums, unroll=True)
        for q, now in enumerate(sums):
            folded[8 * q : 8 * q + 8, :] = now
        for block in range(blocks):
            buffer[last_row + 1 : last_row + 2, PAD + block * 128 : PAD + block * 128 + 128] = folded[block : block + 1, :]

    def fold_at(strip, buffer, last_row):
        @pl.when(tile == strip)
        def _():
            fold(buffer, last_row)

    first, second = ROUNDS
    halo_wait(quarter_mask, mask_recv, True)

    def pack_mask(block, carry):
        at = pl.multiple_of(block * 128, 128)
        packed_mask[:, pl.ds(at, 128)] = packed(quarter_mask[0:24, pl.ds(at, 128)])
        return carry

    lax.fori_loop(0, blocks, pack_mask, 0, unroll=8)
    halo_wait(field, halo_recv, True)

    def apply_mask(block, carry):
        at = pl.multiple_of(block * 128, 128)
        masked[:, pl.ds(at + PAD, 128)] = (4.0 * quarter_mask[:, pl.ds(at, 128)]) * field[:, pl.ds(at, 128)]
        return carry

    lax.fori_loop(0, blocks, apply_mask, 0, unroll=8)
    wrap(masked, 32, columns)
    source = masked
    for j in range(first):
        fold_at(top, source, 15)
        if j < 2:
            fold_at(top - 1, source, 23)
        operator(source, v_chain[j], quarter_mask, columns, SHIFTS[j], 32 if j == 0 else 24, 32 if j < 2 else 24)
        source = v_chain[j]

    def of(buffer, rows, pad):
        return lambda block: buffer[rows, pl.ds(pl.multiple_of(block * 128 + pad, 128), 128)]

    def reduce_over_tiles(index):
        def send(d, carry):
            pltpu.make_async_remote_copy(
                src_ref=message.at[index],
                dst_ref=received.at[index, tile],
                send_sem=sum_send.at[index],
                recv_sem=sum_recv.at[index],
                device_id={"tile": lax.rem(tile + d, tiles)},
                device_id_type=MESH,
            ).start()
            return carry

        lax.fori_loop(1, tiles, send, 0, unroll=True)

    def sum_over_tiles(index):
        others = received.at[index, 0 : tiles - 1]
        pltpu.make_async_copy(others, others, sum_recv.at[index]).wait()
        return jnp.sum(received[index], axis=0)

    shared = gram_message([of(field, OWN, 0)] + [of(v, OWN, PAD) for v in v_chain], columns)
    message[0] = shared
    received[0, tile] = shared
    reduce_over_tiles(0)
    diffusivity = h_diffusivity[0, 0]
    x_first, r_next, d_next = coefficient_cg(sum_over_tiles(0), (first + 1,), diffusivity, first, False)

    def next_round(block, carry):
        at = pl.multiple_of(block * 128, 128)
        rows = slice(0, 24)
        held = [field[rows, pl.ds(at, 128)]] + [v[rows, pl.ds(at + PAD, 128)] for v in v_chain]
        mask = 4.0 * quarter_mask[rows, pl.ds(at, 128)]
        for masked_one, own, numbers in ((masked_r, r_own, r_next), (masked_p, p_own, d_next)):
            tall = [jnp.concatenate([numbers[j]] * 3, axis=0) for j in numbers]
            value = tree_sum(number * held[j] for number, j in zip(tall, numbers))
            masked_one[:, pl.ds(at + PAD, 128)] = mask * value
            own[:, pl.ds(at, 128)] = value[8:16]
        return carry

    lax.fori_loop(0, blocks, next_round, 0, unroll=8)
    wrap(masked_r, 24, columns)
    wrap(masked_p, 24, columns)

    for start, chain, length in ((masked_p, p_chain, second), (masked_r, r_chain, second - 1)):
        source = start
        for j in range(length):
            fold_at(top, source, 15 if j == 0 else 7)
            rows, loaded = 8 if j == length - 1 else 16, 24 if j == 0 else 16
            operator(source, chain[j], packed_mask, columns, SHIFTS[j], rows, loaded, pack=j == 0)
            source = chain[j]
    strip_rows = slice(0, 8)
    p_basis = [of(p_own, strip_rows, 0)] + [of(p, strip_rows, PAD) for p in p_chain]
    r_basis = [of(r_own, strip_rows, 0)] + [of(r, strip_rows, PAD) for r in r_chain]
    shared = gram_message(p_basis + r_basis, columns)
    message[1] = shared
    received[1, tile] = shared
    reduce_over_tiles(1)
    v_basis = [of(field, OWN, 0)] + [of(v, OWN, PAD) for v in v_chain]

    def part_one(block, carry):
        at = pl.multiple_of(block * 128, 128)
        result[:, pl.ds(at, 128)] = tree_sum(x_first[j] * v_basis[j](block) for j in x_first)
        return carry

    lax.fori_loop(0, blocks, part_one, 0, unroll=8)
    x_second, _, _ = coefficient_cg(sum_over_tiles(1), (second + 1, second), diffusivity, second, True)

    basis = p_basis + r_basis
    pieces = 4
    width = columns // pieces
    for piece in range(pieces):

        def part_two(block, carry, piece=piece):
            block = block + piece * (width // 128)
            at = pl.multiple_of(block * 128, 128)
            result[:, pl.ds(at, 128)] += tree_sum(x_second[j] * basis[j](block) for j in x_second)
            return carry

        lax.fori_loop(0, width // 128, part_two, 0, unroll=True)
        here = slice(piece * width, piece * width + width)
        pltpu.make_async_remote_copy(
            src_ref=result.at[:, here],
            dst_ref=other_out.at[:, here],
            send_sem=last_send,
            recv_sem=last_recv,
            device_id={"var": 1 - var},
            device_id_type=MESH,
        ).start()
    keep = pltpu.make_async_copy(result, solved_out, last_local)
    keep.start()

    def sent(buffer, sem):
        pltpu.make_async_copy(buffer, buffer, sem).wait()

    sent(rhs.at[0 : levels - 1], there_send)
    sent(rhs.at[0 : levels - 1], back_send)
    halo_wait(quarter_mask, mask_send, False)
    halo_wait(field, halo_send, False)
    for index in range(2):
        sent(received.at[index, 0 : tiles - 1], sum_send.at[index])
    keep.wait()
    sent(result, last_send)
    pltpu.make_async_copy(other_out, other_out, last_recv).wait()


def per_device(
    background, norm_factor, v_diffusivity, h_diffusivity, sea_mask, fold_order, coupling
):
    rows, columns = background.shape[2:]
    levels, tiles = lax.axis_size("lev"), lax.axis_size("tile")
    part = columns // levels
    f32 = jnp.float32
    strip = jax.ShapeDtypeStruct((rows, columns), f32)
    vmem = pltpu.VMEM
    tall = vmem((32, columns), f32)

    def padded(height):
        return vmem((height, columns + 2 * PAD), f32)

    first, second = ROUNDS
    blocks = columns // 128
    dma = pltpu.SemaphoreType.DMA
    in_hbm = functools.partial(pltpu.with_memory_space_constraint, memory_space=pltpu.HBM)
    solved, other = pl.pallas_call(
        kernel,
        out_shape=(strip, strip),
        in_specs=[pl.BlockSpec(memory_space=pl.ANY)] * 3
        + [pl.BlockSpec(memory_space=pltpu.SMEM)]
        + [pl.BlockSpec(memory_space=pl.ANY)] * 2,
        out_specs=(pl.BlockSpec(memory_space=pl.ANY),) * 2,
        scratch_shapes=[
            vmem((rows, columns), f32),
            vmem((rows, columns), f32),
            vmem((levels, rows, part), f32),
            vmem((rows, columns), jnp.int32),
            vmem((1, columns), jnp.int32),
            vmem((rows, columns), f32),
            vmem((levels, rows, part), f32),
            vmem((levels, rows, part), f32),
            vmem((levels, rows, part), f32),
            vmem((levels, rows, part), f32),
            vmem((levels, rows, part), f32),
            tall,
            tall,
            vmem((16, columns), f32),
            padded(32),
            [padded(32 if j == 0 else 24) for j in range(first)],
            [padded(16)] * second,
            [padded(16)] * (second - 1),
            padded(24),
            padded(24),
            vmem((rows, columns), f32),
            vmem((rows, columns), f32),
            vmem((blocks, 128), jnp.int32),
            vmem((blocks, 128), jnp.int32),
            vmem((blocks, 128), f32),
            vmem((2, 1, 128), f32),
            vmem((2, tiles, 1, 128), f32),
            vmem((rows, columns), f32),
            dma((5,)),
            dma,
            dma,
            dma,
            dma((levels,)),
            dma((4,)),
            dma((4,)),
            dma((4,)),
            dma((4,)),
            dma((2,)),
            dma((2,)),
            dma,
            dma,
            dma,
        ],
        compiler_params=pltpu.CompilerParams(
            collective_id=0, has_side_effects=True, vmem_limit_bytes=40 * 2**20
        ),
    )(
        in_hbm(background.reshape(rows, columns)),
        in_hbm(norm_factor.reshape(rows, columns)),
        in_hbm(v_diffusivity.reshape(levels, rows, part)),
        h_diffusivity,
        in_hbm(sea_mask.reshape(rows, columns)),
        in_hbm(fold_order.reshape(1, columns)),
    )
    return (solved + coupling[0, 0] * other)[None, None]


def solution(mesh):
    placed = (
        P("var", "lev", "tile", None),
        P("var", "lev", "tile", None),
        P("var", None, "tile", "lev"),
        P("var", "lev"),
        P("lev", "tile", None),
        P(),
        P("var", "lev", "tile", None),
    )
    return jax.shard_map(
        per_device,
        mesh=mesh,
        in_specs=placed,
        out_specs=P("var", "lev", "tile", None),
        check_vma=False,
    )
```

time: 61.7 us -> 58.2 us (0.943)
  Pallas kernels: 60.2 us -> 56.7 us
    pallas_call x1, Pallas kernels: 60.2 us -> 56.7 us  [per_device(): pl.pallas_call(kernel, out_shape=(strip, strip), in_specs=[pl.BlockSpec(m...]
where the time goes in v4:
time: 58.2 us; the launch traced here: 58.1 us
  Pallas kernels  56.7 us (97%)
  other arithmetic  0.68 us (1%)
  between operations  0.68 us (1%)
    pallas_call x1, Pallas kernels, per_device(): pl.pallas_call(kernel, out_shape=(strip, strip), in_specs=[pl.BlockSpec(m...  56.7 us

profile of v4, /device:TPU:8, one launch (start us, length us, event | category | flops | bytes accessed | tf_op | source)
XLA Modules:
  0.0 58.1 jit_solution(16014745967341260925)
XLA Ops:
  0.7 0.0 copy-start
  0.7 56.7 %shard_map.73 = (f32[8,4096]{1,0:T(8,128)S(1)}, f32[8,4096]{1,0:T(8,128)S(1)}) custom-call(f32[8,4096]{1,0:T(8,128)} %bitcast.13, f32[8,4096]{1,0:T(8,128)} %bitcast.14, f32[8,8,512]{2,1,0:T(8,128)} %bitcast.15, f32[1,1]{1,0:T(1,128)S(6)} %copy.8.h_diffusivity, s32[8,4096]{1,0:T(8,128)} %bitcast.16, s32[1,4096]{1,0:T(1,128)} %bitcast.17), custom_call_target="tpu_custom_call" | custom-call | tf_op jit(solution)/shard_map/pallas_call | solution.py:462
  57.4 0.0 copy-done
  57.4 0.7 %fusion.1 = f32[1,1,8,4096]{3,2,1,0:T(8,128)} fusion(f32[8,4096]{1,0:T(8,128)S(1)} %get-tuple-element.7, f32[8,4096]{1,0:T(8,128)S(1)} %get-tuple-element.8, f32[1,1,8,4096]{3,2,1,0:T(8,128)S(1)} %copy-done), kind=kLoop, calls=%fused_computation.2 | loop fusion | flops 65536 | bytes 524288 | tf_op jit(solution)/shard_map/broadcast_in_dim | solution.py:524
Async XLA Ops:
  0.7 56.7 %copy-start = (f32[1,1,8,4096]{3,2,1,0:T(8,128)S(1)}, f32[1,1,8,4096]{3,2,1,0:T(8,128)}, u32[]{:S(2)}) copy-start(f32[1,1,8,4096]{3,2,1,0:T(8,128)} %param.13) | copy-start | bytes 393220

commit v5 on v4

--- a/solution.py
+++ b/solution.py
@@ -133,9 +133,9 @@
     solved_out, other_out,
     bg, nf, vd, mask_in, fold_in, scaled, rhs, solved, inverse, below, upper,
     field, quarter_mask, packed_mask, masked, v_chain, p_chain, r_chain, masked_p, masked_r, p_own, r_own,
-    partner_row, partner_lane, folded, message, received, result,
+    partner_row, partner_lane, folded, message, near, total, far, result,
     load_sem, there_send, there_recv, back_send, back_recv,
-    halo_send, halo_recv, mask_send, mask_recv, sum_send, sum_recv, last_send, last_recv, last_local,
+    halo_send, halo_recv, mask_send, mask_recv, near_send, near_recv, far_send, far_recv, last_send, last_recv, last_local,
 ):
     tile, lev, var = (lax.axis_index(a) for a in ("tile", "lev", "var"))
     tiles, levels = lax.axis_size("tile"), lax.axis_size("lev")
@@ -163,20 +163,24 @@
 
     peers = [peer_level(d) for d in range(levels)]
 
-    def greet_tile(d, carry):
-        pl.semaphore_signal(barrier, inc=1, device_id={"tile": lax.rem(tile + d, tiles)}, device_id_type=MESH)
-        return carry
+    across = 8
+    run, place = tile // across, lax.rem(tile, across)
+    in_run = [across * run + lax.rem(place + d, across) for d in range(across)]
+    over_runs = [lax.rem(tile + across * d, tiles) for d in range(tiles // across)]
+    beside = [lax.rem(tile + d + tiles, tiles) for d in (1, -1, 2, -2)]
 
     for d in range(1, levels):
         pl.semaphore_signal(barrier, inc=1, device_id={"lev": peers[d]}, device_id_type=MESH)
     pl.semaphore_signal(barrier, inc=1, device_id={"var": 1 - var}, device_id_type=MESH)
-    lax.fori_loop(1, tiles, greet_tile, 0, unroll=True)
+    strips = beside + in_run[1:] + over_runs[1:]
+    for to in strips:
+        pl.semaphore_signal(barrier, inc=1, device_id={"tile": to}, device_id_type=MESH)
     loads[0].wait()
     loads[1].wait()
     scaled[...] = nf[...] * bg[...]
     loads[2].wait()
     quarter_mask[OWN, :] = 0.25 * mask_in[...].astype(f32)
-    pl.semaphore_wait(barrier, (levels - 1) + (tiles - 1) + 1)
+    pl.semaphore_wait(barrier, (levels - 1) + len(strips) + 1)
 
     for d in reversed(range(1, levels)):
         pltpu.make_async_remote_copy(
@@ -337,29 +341,36 @@
     def of(buffer, rows, pad):
         return lambda block: buffer[rows, pl.ds(pl.multiple_of(block * 128 + pad, 128), 128)]
 
-    def reduce_over_tiles(index):
-        def send(d, carry):
+    def send_sums(message, received, peers_here, own_slot, send, recv):
+        for to in peers_here[1:]:
             pltpu.make_async_remote_copy(
-                src_ref=message.at[index],
-                dst_ref=received.at[index, tile],
-                send_sem=sum_send.at[index],
-                recv_sem=sum_recv.at[index],
-                device_id={"tile": lax.rem(tile + d, tiles)},
+                src_ref=message,
+                dst_ref=received.at[own_slot],
+                send_sem=send,
+                recv_sem=recv,
+                device_id={"tile": to},
                 device_id_type=MESH,
             ).start()
-            return carry
-
-        lax.fori_loop(1, tiles, send, 0, unroll=True)
+
+    def take_sums(received, recv):
+        others = received.at[0 : received.shape[0] - 1]
+        pltpu.make_async_copy(others, others, recv).wait()
+        return jnp.sum(received[...], axis=0)
+
+    def reduce_over_tiles(index, shared):
+        message[index] = shared
+        near[index, place] = shared
+        send_sums(message.at[index], near.at[index], in_run, place, near_send.at[index], near_recv.at[index])
 
     def sum_over_tiles(index):
-        others = received.at[index, 0 : tiles - 1]
-        pltpu.make_async_copy(others, others, sum_recv.at[index]).wait()
-        return jnp.sum(received[index], axis=0)
+        shared = take_sums(near.at[index], near_recv.at[index])
+        total[index] = shared
+        far[index, run] = shared
+        send_sums(total.at[index], far.at[index], over_runs, run, far_send.at[index], far_recv.at[index])
+        return take_sums(far.at[index], far_recv.at[index])
 
     shared = gram_message([of(field, OWN, 0)] + [of(v, OWN, PAD) for v in v_chain], columns)
-    message[0] = shared
-    received[0, tile] = shared
-    reduce_over_tiles(0)
+    reduce_over_tiles(0, shared)
     diffusivity = h_diffusivity[0, 0]
     x_first, r_next, d_next = coefficient_cg(sum_over_tiles(0), (first + 1,), diffusivity, first, False)
 
@@ -390,9 +401,7 @@
     p_basis = [of(p_own, strip_rows, 0)] + [of(p, strip_rows, PAD) for p in p_chain]
     r_basis = [of(r_own, strip_rows, 0)] + [of(r, strip_rows, PAD) for r in r_chain]
     shared = gram_message(p_basis + r_basis, columns)
-    message[1] = shared
-    received[1, tile] = shared
-    reduce_over_tiles(1)
+    reduce_over_tiles(1, shared)
     v_basis = [of(field, OWN, 0)] + [of(v, OWN, PAD) for v in v_chain]
 
     def part_one(block, carry):
@@ -435,7 +444,8 @@
     halo_wait(quarter_mask, mask_send, False)
     halo_wait(field, halo_send, False)
     for index in range(2):
-        sent(received.at[index, 0 : tiles - 1], sum_send.at[index])
+        sent(near.at[index, 0 : across - 1], near_send.at[index])
+        sent(far.at[index, 0 : tiles // across - 1], far_send.at[index])
     keep.wait()
     sent(result, last_send)
     pltpu.make_async_copy(other_out, other_out, last_recv).wait()
@@ -493,7 +503,9 @@
             vmem((blocks, 128), jnp.int32),
             vmem((blocks, 128), f32),
             vmem((2, 1, 128), f32),
-            vmem((2, tiles, 1, 128), f32),
+            vmem((2, 8, 1, 128), f32),
+            vmem((2, 1, 128), f32),
+            vmem((2, tiles // 8, 1, 128), f32),
             vmem((rows, columns), f32),
             dma((5,)),
             dma,
@@ -504,6 +516,8 @@
             dma((4,)),
             dma((4,)),
             dma((4,)),
+            dma((2,)),
+            dma((2,)),
             dma((2,)),
             dma((2,)),
             dma,

time: 58.2 us -> 59.8 us (1.027)
  the two profiles are of different devices: /device:TPU:8 before, /device:TPU:64 now
where the time goes in v5:
time: 59.8 us; the launch traced here: 59.7 us
  Pallas kernels  58.3 us (97%)
  other arithmetic  0.68 us (1%)
  between operations  0.68 us (1%)
    pallas_call x1, Pallas kernels, per_device(): pl.pallas_call(kernel, out_shape=(strip, strip), in_specs=[pl.BlockSpec(m...  58.3 us

profile of v5, /device:TPU:64, one launch (start us, length us, event | category | flops | bytes accessed | tf_op | source)
XLA Modules:
  0.0 59.7 jit_solution(4407682827204597465)
XLA Ops:
  0.7 0.0 copy-start
  0.7 58.3 %shard_map.73 = (f32[8,4096]{1,0:T(8,128)S(1)}, f32[8,4096]{1,0:T(8,128)S(1)}) custom-call(f32[8,4096]{1,0:T(8,128)} %bitcast.13, f32[8,4096]{1,0:T(8,128)} %bitcast.14, f32[8,8,512]{2,1,0:T(8,128)} %bitcast.15, f32[1,1]{1,0:T(1,128)S(6)} %copy.8.h_diffusivity, s32[8,4096]{1,0:T(8,128)} %bitcast.16, s32[1,4096]{1,0:T(1,128)} %bitcast.17), custom_call_target="tpu_custom_call" | custom-call | tf_op jit(solution)/shard_map/pallas_call | solution.py:472
  59.0 0.0 copy-done
  59.0 0.7 %fusion.1 = f32[1,1,8,4096]{3,2,1,0:T(8,128)} fusion(f32[8,4096]{1,0:T(8,128)S(1)} %get-tuple-element.7, f32[8,4096]{1,0:T(8,128)S(1)} %get-tuple-element.8, f32[1,1,8,4096]{3,2,1,0:T(8,128)S(1)} %copy-done), kind=kLoop, calls=%fused_computation.2 | loop fusion | flops 65536 | bytes 524288 | tf_op jit(solution)/shard_map/broadcast_in_dim | solution.py:538
Async XLA Ops:
  0.7 58.3 %copy-start = (f32[1,1,8,4096]{3,2,1,0:T(8,128)S(1)}, f32[1,1,8,4096]{3,2,1,0:T(8,128)}, u32[]{:S(2)}) copy-start(f32[1,1,8,4096]{3,2,1,0:T(8,128)} %param.13) | copy-start | bytes 393220

commit v6 on v4

--- a/solution.py
+++ b/solution.py
@@ -93,8 +93,11 @@
     return jnp.concatenate([tall[8:16], jnp.where(upper_half, tall[16:24], tall[0:8])], axis=0)
 
 
-def operator(source, target, quarter_mask, columns, shift, rows, loaded, pack=False, group=8):
+def operator(source, target, quarter_mask, columns, shift, rows, loaded, pack=False, folded=None, group=8):
     lane = lax.broadcasted_iota(jnp.int32, (rows, 128), 1)
+    if folded is not None:
+        line, last_row = folded
+        is_last = lax.broadcasted_iota(jnp.int32, (rows, 128), 0) == last_row
     cut = packed if pack else lambda value: value[0:rows]
 
     def body(chunk, carry):
@@ -111,6 +114,8 @@
             west = jnp.where(lane == 0, behind[k - 2], behind[k - 1])
             north = cut(pltpu.roll(here, loaded - 1, 0))
             south = cut(pltpu.roll(here, 1, 0))
+            if folded is not None:
+                north = jnp.where(is_last, line[pl.ds(chunk * group + k - 2, 1), :], north)
             here = cut(here)
             value = 4.0 * here - ((north + south) + (east + west))
             value = quarter_mask[0:rows, pl.ds(at + 128 * (k - 2), 128)] * value
@@ -133,7 +138,7 @@
     solved_out, other_out,
     bg, nf, vd, mask_in, fold_in, scaled, rhs, solved, inverse, below, upper,
     field, quarter_mask, packed_mask, masked, v_chain, p_chain, r_chain, masked_p, masked_r, p_own, r_own,
-    partner_row, partner_lane, folded, message, received, result,
+    partner_row, partner_lane, lines, folded_p, folded_r, message, received, result,
     load_sem, there_send, there_recv, back_send, back_recv,
     halo_send, halo_recv, mask_send, mask_recv, sum_send, sum_recv, last_send, last_recv, last_local,
 ):
@@ -223,6 +228,11 @@
         def _(land=land, rows=high - low):
             for buffer in (field, quarter_mask):
                 buffer[land : land + rows, :] = jnp.zeros((rows, columns), f32)
+
+    @pl.when(tile == top)
+    def _():
+        for chain in v_chain[1:]:
+            chain[16:24, :] = jnp.zeros((8, chain.shape[1]), f32)
 
     loads[3].wait()
     above = jnp.zeros((ROWS, part), f32)
@@ -276,37 +286,32 @@
             device_id_type=MESH,
         ).start()
     field[OWN, pl.ds(my_columns, part)] = solved[lev]
-    halo_copies(field, halo_send, halo_recv, my_columns, part)
-
     for d in range(1, levels):
         at = pl.multiple_of(peers[d] * part, part)
         here = field.at[OWN, pl.ds(at, part)]
         pltpu.make_async_copy(here, here, back_recv.at[d]).wait()
-        halo_copies(field, halo_send, halo_recv, at, part)
-
-    def fold(buffer, last_row):
-        sums = tuple(jnp.zeros((8, 128), f32) for _ in range(blocks // 8))
-
-        def pick(block, sums):
+        if d % 2 == 1:
+            at = pl.multiple_of(peers[d] // 2 * (2 * part), 2 * part)
+            halo_copies(field, halo_send, halo_recv, at, 2 * part)
+
+    def fold(buffer, last_row, folded):
+        def repeat(block, carry):
             at = pl.multiple_of(PAD + block * 128, 128)
-            line = jnp.broadcast_to(buffer[last_row : last_row + 1, pl.ds(at, 128)], (8, 128))
-            chosen = []
-            for q, now in enumerate(sums):
-                rows = slice(8 * q, 8 * q + 8)
-                moved = jnp.take_along_axis(line, partner_lane[rows, :], axis=1)
-                chosen.append(jnp.where(partner_row[rows, :] == block, moved, now))
-            return tuple(chosen)
-
-        sums = lax.fori_loop(0, blocks, pick, sums, unroll=True)
-        for q, now in enumerate(sums):
-            folded[8 * q : 8 * q + 8, :] = now
-        for block in range(blocks):
-            buffer[last_row + 1 : last_row + 2, PAD + block * 128 : PAD + block * 128 + 128] = folded[block : block + 1, :]
-
-    def fold_at(strip, buffer, last_row):
-        @pl.when(tile == strip)
-        def _():
-            fold(buffer, last_row)
+            lines[block] = jnp.broadcast_to(buffer[last_row : last_row + 1, pl.ds(at, 128)], (8, 128))
+            return carry
+
+        lax.fori_loop(0, blocks, repeat, 0, unroll=True)
+        for q in range(blocks // 8):
+            rows = slice(8 * q, 8 * q + 8)
+            at_lane, at_row = partner_lane[rows, :], partner_row[rows, :]
+
+            def pick(block, now, at_lane=at_lane, at_row=at_row):
+                moved = jnp.take_along_axis(lines[block], at_lane, axis=1, mode="promise_in_bounds")
+                return jnp.where(at_row == block, moved, now)
+
+            folded[rows, :] = lax.fori_loop(0, blocks, pick, jnp.zeros((8, 128), f32), unroll=True)
+
+    is_top = tile == top
 
     first, second = ROUNDS
     halo_wait(quarter_mask, mask_recv, True)
@@ -328,10 +333,26 @@
     wrap(masked, 32, columns)
     source = masked
     for j in range(first):
-        fold_at(top, source, 15)
         if j < 2:
-            fold_at(top - 1, source, 23)
-        operator(source, v_chain[j], quarter_mask, columns, SHIFTS[j], 32 if j == 0 else 24, 32 if j < 2 else 24)
+
+            @pl.when(tile == top - 1)
+            def _(source=source):
+                fold(source, 23, folded_p)
+                for block in range(blocks):
+                    at = PAD + block * 128
+                    source[24:25, at : at + 128] = folded_p[block : block + 1, :]
+
+        @pl.when(is_top)
+        def _(source=source, j=j):
+            fold(source, 15, folded_p)
+            rows, loaded = 32 if j == 0 else 16, 32 if j < 2 else 16
+            operator(source, v_chain[j], quarter_mask, columns, SHIFTS[j], rows, loaded, folded=(folded_p, 15))
+
+        @pl.when(jnp.logical_not(is_top))
+        def _(source=source, j=j):
+            rows, loaded = 32 if j == 0 else 24, 32 if j < 2 else 24
+            operator(source, v_chain[j], quarter_mask, columns, SHIFTS[j], rows, loaded)
+
         source = v_chain[j]
 
     def of(buffer, rows, pad):
@@ -379,13 +400,26 @@
     wrap(masked_r, 24, columns)
     wrap(masked_p, 24, columns)
 
-    for start, chain, length in ((masked_p, p_chain, second), (masked_r, r_chain, second - 1)):
-        source = start
-        for j in range(length):
-            fold_at(top, source, 15 if j == 0 else 7)
-            rows, loaded = 8 if j == length - 1 else 16, 24 if j == 0 else 16
-            operator(source, chain[j], packed_mask, columns, SHIFTS[j], rows, loaded, pack=j == 0)
-            source = chain[j]
+    p_source, r_source = masked_p, masked_r
+    for j in range(second):
+        work = [(p_source, p_chain[j], folded_p, 8 if j == second - 1 else 16)]
+        if j < second - 1:
+            work.append((r_source, r_chain[j], folded_r, 8 if j == second - 2 else 16))
+
+        def both(work, j, at_top):
+            if at_top:
+                for source, _, folded, _ in work:
+                    fold(source, 15 if j == 0 else 7, folded)
+            for source, target, folded, rows in work:
+                operator(
+                    source, target, packed_mask, columns, SHIFTS[j], rows, 24 if j == 0 else 16,
+                    pack=j == 0, folded=(folded, 7) if at_top else None,
+                )
+
+        pl.when(is_top)(functools.partial(both, work, j, True))
+        pl.when(jnp.logical_not(is_top))(functools.partial(both, work, j, False))
+        if j < second - 1:
+            p_source, r_source = p_chain[j], r_chain[j]
     strip_rows = slice(0, 8)
     p_basis = [of(p_own, strip_rows, 0)] + [of(p, strip_rows, PAD) for p in p_chain]
     r_basis = [of(r_own, strip_rows, 0)] + [of(r, strip_rows, PAD) for r in r_chain]
@@ -491,6 +525,8 @@
             vmem((rows, columns), f32),
             vmem((blocks, 128), jnp.int32),
             vmem((blocks, 128), jnp.int32),
+            vmem((blocks, 8, 128), f32),
+            vmem((blocks, 128), f32),
             vmem((blocks, 128), f32),
             vmem((2, 1, 128), f32),
             vmem((2, tiles, 1, 128), f32),

time: 58.2 us -> 55.8 us (0.959)
  Pallas kernels: 56.7 us -> 54.4 us
    pallas_call x1, Pallas kernels: 56.7 us -> 54.4 us  [per_device(): pl.pallas_call(kernel, out_shape=(strip, strip), in_specs=[pl.BlockSpec(m...]
where the time goes in v6:
time: 55.8 us; the launch traced here: 55.7 us
  Pallas kernels  54.4 us (97%)
  other arithmetic  0.68 us (1%)
  between operations  0.68 us (1%)
    pallas_call x1, Pallas kernels, per_device(): pl.pallas_call(kernel, out_shape=(strip, strip), in_specs=[pl.BlockSpec(m...  54.4 us

profile of v6, /device:TPU:8, one launch (start us, length us, event | category | flops | bytes accessed | tf_op | source)
XLA Modules:
  0.0 55.7 jit_solution(17820208286305982109)
XLA Ops:
  0.7 0.0 copy-start
  0.7 54.4 %shard_map.73 = (f32[8,4096]{1,0:T(8,128)S(1)}, f32[8,4096]{1,0:T(8,128)S(1)}) custom-call(f32[8,4096]{1,0:T(8,128)} %bitcast.13, f32[8,4096]{1,0:T(8,128)} %bitcast.14, f32[8,8,512]{2,1,0:T(8,128)} %bitcast.15, f32[1,1]{1,0:T(1,128)S(6)} %copy.8.h_diffusivity, s32[8,4096]{1,0:T(8,128)} %bitcast.16, s32[1,4096]{1,0:T(1,128)} %bitcast.17), custom_call_target="tpu_custom_call" | custom-call | tf_op jit(solution)/shard_map/pallas_call | solution.py:496
  55.0 0.0 copy-done
  55.0 0.7 %fusion.1 = f32[1,1,8,4096]{3,2,1,0:T(8,128)} fusion(f32[8,4096]{1,0:T(8,128)S(1)} %get-tuple-element.7, f32[8,4096]{1,0:T(8,128)S(1)} %get-tuple-element.8, f32[1,1,8,4096]{3,2,1,0:T(8,128)S(1)} %copy-done), kind=kLoop, calls=%fused_computation.2 | loop fusion | flops 65536 | bytes 524288 | tf_op jit(solution)/shard_map/broadcast_in_dim | solution.py:560
Async XLA Ops:
  0.7 54.4 %copy-start = (f32[1,1,8,4096]{3,2,1,0:T(8,128)S(1)}, f32[1,1,8,4096]{3,2,1,0:T(8,128)}, u32[]{:S(2)}) copy-start(f32[1,1,8,4096]{3,2,1,0:T(8,128)} %param.13) | copy-start | bytes 393220

commit v7 on v6

--- a/solution.py
+++ b/solution.py
@@ -124,7 +124,7 @@
             target[0:rows, pl.ds(at + 128 * (k - 1), 128)] = value
         return carry
 
-    lax.fori_loop(0, columns // (group * 128), body, 0, unroll=True)
+    lax.fori_loop(0, columns // (group * 128), body, 0)
     wrap(target, rows, columns)
 
 

time: 55.8 us -> 59.6 us (1.068)
  Pallas kernels: 54.4 us -> 58.1 us
    pallas_call x1, Pallas kernels: 54.4 us -> 58.1 us  [per_device(): pl.pallas_call(kernel, out_shape=(strip, strip), in_specs=[pl.BlockSpec(m...]
where the time goes in v7:
time: 59.6 us; the launch traced here: 59.5 us
  Pallas kernels  58.1 us (97%)
  other arithmetic  0.68 us (1%)
  between operations  0.68 us (1%)
    pallas_call x1, Pallas kernels, per_device(): pl.pallas_call(kernel, out_shape=(strip, strip), in_specs=[pl.BlockSpec(m...  58.1 us

profile of v7, /device:TPU:8, one launch (start us, length us, event | category | flops | bytes accessed | tf_op | source)
XLA Modules:
  0.0 59.5 jit_solution(2543891091386770326)
XLA Ops:
  0.7 0.0 copy-start
  0.7 58.1 %shard_map.73 = (f32[8,4096]{1,0:T(8,128)S(1)}, f32[8,4096]{1,0:T(8,128)S(1)}) custom-call(f32[8,4096]{1,0:T(8,128)} %bitcast.13, f32[8,4096]{1,0:T(8,128)} %bitcast.14, f32[8,8,512]{2,1,0:T(8,128)} %bitcast.15, f32[1,1]{1,0:T(1,128)S(6)} %copy.8.h_diffusivity, s32[8,4096]{1,0:T(8,128)} %bitcast.16, s32[1,4096]{1,0:T(1,128)} %bitcast.17), custom_call_target="tpu_custom_call" | custom-call | tf_op jit(solution)/shard_map/pallas_call | solution.py:496
  58.8 0.0 copy-done
  58.8 0.7 %fusion.1 = f32[1,1,8,4096]{3,2,1,0:T(8,128)} fusion(f32[8,4096]{1,0:T(8,128)S(1)} %get-tuple-element.7, f32[8,4096]{1,0:T(8,128)S(1)} %get-tuple-element.8, f32[1,1,8,4096]{3,2,1,0:T(8,128)S(1)} %copy-done), kind=kLoop, calls=%fused_computation.2 | loop fusion | flops 65536 | bytes 524288 | tf_op jit(solution)/shard_map/broadcast_in_dim | solution.py:560
Async XLA Ops:
  0.7 58.2 %copy-start = (f32[1,1,8,4096]{3,2,1,0:T(8,128)S(1)}, f32[1,1,8,4096]{3,2,1,0:T(8,128)}, u32[]{:S(2)}) copy-start(f32[1,1,8,4096]{3,2,1,0:T(8,128)} %param.13) | copy-start | bytes 393220

commit v8 on v6

--- a/solution.py
+++ b/solution.py
@@ -39,7 +39,7 @@
             return tuple(total + held[i] * held[j] for total, (i, j) in zip(sums, group))
 
         zeros = tuple(jnp.zeros((8, 128), jnp.float32) for _ in group)
-        sums = lax.fori_loop(0, columns // 128, body, zeros, unroll=8)
+        sums = lax.fori_loop(0, columns // 128, body, zeros, unroll=True)
         for place, total in enumerate(sums):
             message = jnp.where(lane == at + place, jnp.sum(total, axis=1, keepdims=True), message)
     return jnp.sum(message, axis=0, keepdims=True)
@@ -321,7 +321,7 @@
         packed_mask[:, pl.ds(at, 128)] = packed(quarter_mask[0:24, pl.ds(at, 128)])
         return carry
 
-    lax.fori_loop(0, blocks, pack_mask, 0, unroll=8)
+    lax.fori_loop(0, blocks, pack_mask, 0, unroll=True)
     halo_wait(field, halo_recv, True)
 
     def apply_mask(block, carry):
@@ -329,31 +329,27 @@
         masked[:, pl.ds(at + PAD, 128)] = (4.0 * quarter_mask[:, pl.ds(at, 128)]) * field[:, pl.ds(at, 128)]
         return carry
 
-    lax.fori_loop(0, blocks, apply_mask, 0, unroll=8)
+    lax.fori_loop(0, blocks, apply_mask, 0, unroll=True)
     wrap(masked, 32, columns)
-    source = masked
-    for j in range(first):
-        if j < 2:
-
-            @pl.when(tile == top - 1)
-            def _(source=source):
+    def first_chain(strip):
+        source = masked
+        for j in range(first):
+            folded, rows = None, 24
+            if strip == "top":
+                fold(source, 15, folded_p)
+                folded, rows = (folded_p, 15), 16
+            elif strip == "next" and j < 2:
                 fold(source, 23, folded_p)
                 for block in range(blocks):
                     at = PAD + block * 128
                     source[24:25, at : at + 128] = folded_p[block : block + 1, :]
-
-        @pl.when(is_top)
-        def _(source=source, j=j):
-            fold(source, 15, folded_p)
-            rows, loaded = 32 if j == 0 else 16, 32 if j < 2 else 16
-            operator(source, v_chain[j], quarter_mask, columns, SHIFTS[j], rows, loaded, folded=(folded_p, 15))
-
-        @pl.when(jnp.logical_not(is_top))
-        def _(source=source, j=j):
-            rows, loaded = 32 if j == 0 else 24, 32 if j < 2 else 24
-            operator(source, v_chain[j], quarter_mask, columns, SHIFTS[j], rows, loaded)
-
-        source = v_chain[j]
+            if j == 0:
+                rows = 32
+            operator(
+                source, v_chain[j], quarter_mask, columns, SHIFTS[j], rows, 32 if j < 2 else rows, folded=folded
+            )
+            source = v_chain[j]
+        message[0] = gram_message([of(field, OWN, 0)] + [of(v, OWN, PAD) for v in v_chain], columns)
 
     def of(buffer, rows, pad):
         return lambda block: buffer[rows, pl.ds(pl.multiple_of(block * 128 + pad, 128), 128)]
@@ -377,9 +373,10 @@
         pltpu.make_async_copy(others, others, sum_recv.at[index]).wait()
         return jnp.sum(received[index], axis=0)
 
-    shared = gram_message([of(field, OWN, 0)] + [of(v, OWN, PAD) for v in v_chain], columns)
-    message[0] = shared
-    received[0, tile] = shared
+    pl.when(is_top)(functools.partial(first_chain, "top"))
+    pl.when(tile == top - 1)(functools.partial(first_chain, "next"))
+    pl.when(tile < top - 1)(functools.partial(first_chain, "other"))
+    received[0, tile] = message[0]
     reduce_over_tiles(0)
     diffusivity = h_diffusivity[0, 0]
     x_first, r_next, d_next = coefficient_cg(sum_over_tiles(0), (first + 1,), diffusivity, first, False)
@@ -396,17 +393,20 @@
             own[:, pl.ds(at, 128)] = value[8:16]
         return carry
 
-    lax.fori_loop(0, blocks, next_round, 0, unroll=8)
+    lax.fori_loop(0, blocks, next_round, 0, unroll=True)
     wrap(masked_r, 24, columns)
     wrap(masked_p, 24, columns)
 
-    p_source, r_source = masked_p, masked_r
-    for j in range(second):
-        work = [(p_source, p_chain[j], folded_p, 8 if j == second - 1 else 16)]
-        if j < second - 1:
-            work.append((r_source, r_chain[j], folded_r, 8 if j == second - 2 else 16))
-
-        def both(work, j, at_top):
+    strip_rows = slice(0, 8)
+    p_basis = [of(p_own, strip_rows, 0)] + [of(p, strip_rows, PAD) for p in p_chain]
+    r_basis = [of(r_own, strip_rows, 0)] + [of(r, strip_rows, PAD) for r in r_chain]
+
+    def second_chains(at_top):
+        sources = [masked_p, masked_r]
+        for j in range(second):
+            work = [(sources[0], p_chain[j], folded_p, 8 if j == second - 1 else 16)]
+            if j < second - 1:
+                work.append((sources[1], r_chain[j], folded_r, 8 if j == second - 2 else 16))
             if at_top:
                 for source, _, folded, _ in work:
                     fold(source, 15 if j == 0 else 7, folded)
@@ -415,17 +415,12 @@
                     source, target, packed_mask, columns, SHIFTS[j], rows, 24 if j == 0 else 16,
                     pack=j == 0, folded=(folded, 7) if at_top else None,
                 )
-
-        pl.when(is_top)(functools.partial(both, work, j, True))
-        pl.when(jnp.logical_not(is_top))(functools.partial(both, work, j, False))
-        if j < second - 1:
-            p_source, r_source = p_chain[j], r_chain[j]
-    strip_rows = slice(0, 8)
-    p_basis = [of(p_own, strip_rows, 0)] + [of(p, strip_rows, PAD) for p in p_chain]
-    r_basis = [of(r_own, strip_rows, 0)] + [of(r, strip_rows, PAD) for r in r_chain]
-    shared = gram_message(p_basis + r_basis, columns)
-    message[1] = shared
-    received[1, tile] = shared
+            sources = [target for _, target, _, _ in work]
+        message[1] = gram_message(p_basis + r_basis, columns)
+
+    pl.when(is_top)(functools.partial(second_chains, True))
+    pl.when(jnp.logical_not(is_top))(functools.partial(second_chains, False))
+    received[1, tile] = message[1]
     reduce_over_tiles(1)
     v_basis = [of(field, OWN, 0)] + [of(v, OWN, PAD) for v in v_chain]
 
@@ -434,7 +429,7 @@
         result[:, pl.ds(at, 128)] = tree_sum(x_first[j] * v_basis[j](block) for j in x_first)
         return carry
 
-    lax.fori_loop(0, blocks, part_one, 0, unroll=8)
+    lax.fori_loop(0, blocks, part_one, 0, unroll=True)
     x_second, _, _ = coefficient_cg(sum_over_tiles(1), (second + 1, second), diffusivity, second, True)
 
     basis = p_basis + r_basis

time: 55.8 us -> 55.1 us (0.987)
  Pallas kernels: 54.4 us -> 53.6 us
    pallas_call x1, Pallas kernels: 54.4 us -> 53.6 us  [per_device(): pl.pallas_call(kernel, out_shape=(strip, strip), in_specs=[pl.BlockSpec(m...]
where the time goes in v8:
time: 55.1 us; the launch traced here: 55 us
  Pallas kernels  53.6 us (97%)
  other arithmetic  0.68 us (1%)
  between operations  0.68 us (1%)
    pallas_call x1, Pallas kernels, per_device(): pl.pallas_call(kernel, out_shape=(strip, strip), in_specs=[pl.BlockSpec(m...  53.6 us

profile of v8, /device:TPU:8, one launch (start us, length us, event | category | flops | bytes accessed | tf_op | source)
XLA Modules:
  0.0 55.0 jit_solution(2278447740584540337)
XLA Ops:
  0.7 0.0 copy-start
  0.7 53.6 %shard_map.73 = (f32[8,4096]{1,0:T(8,128)S(1)}, f32[8,4096]{1,0:T(8,128)S(1)}) custom-call(f32[8,4096]{1,0:T(8,128)} %bitcast.13, f32[8,4096]{1,0:T(8,128)} %bitcast.14, f32[8,8,512]{2,1,0:T(8,128)} %bitcast.15, f32[1,1]{1,0:T(1,128)S(6)} %copy.8.h_diffusivity, s32[8,4096]{1,0:T(8,128)} %bitcast.16, s32[1,4096]{1,0:T(1,128)} %bitcast.17), custom_call_target="tpu_custom_call" | custom-call | tf_op jit(solution)/shard_map/pallas_call | solution.py:491
  54.3 0.0 copy-done
  54.3 0.7 %fusion.1 = f32[1,1,8,4096]{3,2,1,0:T(8,128)} fusion(f32[8,4096]{1,0:T(8,128)S(1)} %get-tuple-element.7, f32[8,4096]{1,0:T(8,128)S(1)} %get-tuple-element.8, f32[1,1,8,4096]{3,2,1,0:T(8,128)S(1)} %copy-done), kind=kLoop, calls=%fused_computation.2 | loop fusion | flops 65536 | bytes 524288 | tf_op jit(solution)/shard_map/broadcast_in_dim | solution.py:555
Async XLA Ops:
  0.7 53.6 %copy-start = (f32[1,1,8,4096]{3,2,1,0:T(8,128)S(1)}, f32[1,1,8,4096]{3,2,1,0:T(8,128)}, u32[]{:S(2)}) copy-start(f32[1,1,8,4096]{3,2,1,0:T(8,128)} %param.13) | copy-start | bytes 393220

commit v9 on v8

--- a/solution.py
+++ b/solution.py
@@ -22,12 +22,13 @@
     return terms[0]
 
 
-def pairs_of(count):
-    return [(i, j) for i in range(count) for j in range(i, count)]
-
-
-def gram_message(vectors, columns):
-    pairs = pairs_of(len(vectors))
+def pairs_of(chains, last):
+    count = sum(chains)
+    ends = {sum(chains[: i + 1]) - 1 for i in range(len(chains))} if last else set()
+    return [(i, j) for i in range(count) for j in range(i, count) if not (i in ends and j in ends)]
+
+
+def gram_message(vectors, pairs, columns):
     lane = lax.broadcasted_iota(jnp.int32, (8, 128), 1)
     message = jnp.zeros((8, 128), jnp.float32)
     for at in range(0, len(pairs), 28):
@@ -50,7 +51,7 @@
     first = count - chains[-1]
     totals = jnp.broadcast_to(totals, (8, 128))
     gram = {}
-    for place, (i, j) in enumerate(pairs_of(count)):
+    for place, (i, j) in enumerate(pairs_of(chains, last)):
         gram[i, j] = gram[j, i] = jnp.broadcast_to(totals[:, place : place + 1], (8, 128))
     same, start = {}, 0
     for length in chains:
@@ -75,6 +76,7 @@
     d, r, x = {0: 1.0}, {first: 1.0}, {}
     norm_now = gram[first, first]
     for step in range(steps):
+        inverse_now = jnp.where(norm_now > 1e-37, 1.0 / norm_now, 0.0)
         image = image_of(d)
         energy = product(d, image)
         size = jnp.where(energy > 0, jnp.minimum(norm_now / energy, 1.0), 0.0)
@@ -83,7 +85,7 @@
             break
         r = add(r, -size, image)
         norm_next = jnp.maximum(product(r, r), 0.0)
-        d = add(r, jnp.where(norm_now > 0, norm_next / norm_now, 0.0), d)
+        d = add(r, norm_next * inverse_now, d)
         norm_now = norm_next
     return x, r, d
 
@@ -117,10 +119,9 @@
             if folded is not None:
                 north = jnp.where(is_last, line[pl.ds(chunk * group + k - 2, 1), :], north)
             here = cut(here)
-            value = 4.0 * here - ((north + south) + (east + west))
-            value = quarter_mask[0:rows, pl.ds(at + 128 * (k - 2), 128)] * value
-            if shift:
-                value = value - (0.25 * shift) * here
+            beside = (north + south) + (east + west)
+            value = (1.0 - 0.25 * shift) * here if shift else here
+            value = value - quarter_mask[0:rows, pl.ds(at + 128 * (k - 2), 128)] * beside
             target[0:rows, pl.ds(at + 128 * (k - 1), 128)] = value
         return carry
 
@@ -349,28 +350,35 @@
                 source, v_chain[j], quarter_mask, columns, SHIFTS[j], rows, 32 if j < 2 else rows, folded=folded
             )
             source = v_chain[j]
-        message[0] = gram_message([of(field, OWN, 0)] + [of(v, OWN, PAD) for v in v_chain], columns)
+        message[0] = gram_message([of(field, OWN, 0)] + [of(v, OWN, PAD) for v in v_chain], pairs_of((first + 1,), False), columns)
 
     def of(buffer, rows, pad):
         return lambda block: buffer[rows, pl.ds(pl.multiple_of(block * 128 + pad, 128), 128)]
 
+    across = 8
+    run, place = tile // across, lax.rem(tile, across)
+    away = sorted(
+        ((i, j) for i in range(tiles // across) for j in range(across) if i or j),
+        key=lambda at: -min(at[0], tiles // across - at[0]) - min(at[1], across - at[1]),
+    )
+    others = [
+        across * lax.rem(run + i, tiles // across) + lax.rem(place + j, across) for i, j in away
+    ]
+
     def reduce_over_tiles(index):
-        def send(d, carry):
+        for to in others:
             pltpu.make_async_remote_copy(
                 src_ref=message.at[index],
                 dst_ref=received.at[index, tile],
                 send_sem=sum_send.at[index],
                 recv_sem=sum_recv.at[index],
-                device_id={"tile": lax.rem(tile + d, tiles)},
+                device_id={"tile": to},
                 device_id_type=MESH,
             ).start()
-            return carry
-
-        lax.fori_loop(1, tiles, send, 0, unroll=True)
 
     def sum_over_tiles(index):
-        others = received.at[index, 0 : tiles - 1]
-        pltpu.make_async_copy(others, others, sum_recv.at[index]).wait()
+        all_others = received.at[index, 0 : tiles - 1]
+        pltpu.make_async_copy(all_others, all_others, sum_recv.at[index]).wait()
         return jnp.sum(received[index], axis=0)
 
     pl.when(is_top)(functools.partial(first_chain, "top"))
@@ -416,7 +424,7 @@
                     pack=j == 0, folded=(folded, 7) if at_top else None,
                 )
             sources = [target for _, target, _, _ in work]
-        message[1] = gram_message(p_basis + r_basis, columns)
+        message[1] = gram_message(p_basis + r_basis, pairs_of((second + 1, second), True), columns)
 
     pl.when(is_top)(functools.partial(second_chains, True))
     pl.when(jnp.logical_not(is_top))(functools.partial(second_chains, False))

time: 55.1 us -> 54.8 us (level)
  no operation moved by 1% of the time
where the time goes in v9:
time: 54.8 us; the launch traced here: 54.7 us
  Pallas kernels  53.3 us (97%)
  other arithmetic  0.68 us (1%)
  between operations  0.68 us (1%)
    pallas_call x1, Pallas kernels, per_device(): pl.pallas_call(kernel, out_shape=(strip, strip), in_specs=[pl.BlockSpec(m...  53.3 us

profile of v9, /device:TPU:8, one launch (start us, length us, event | category | flops | bytes accessed | tf_op | source)
XLA Modules:
  0.0 54.7 jit_solution(2426053811182095359)
XLA Ops:
  0.7 0.0 copy-start
  0.7 53.3 %shard_map.73 = (f32[8,4096]{1,0:T(8,128)S(1)}, f32[8,4096]{1,0:T(8,128)S(1)}) custom-call(f32[8,4096]{1,0:T(8,128)} %bitcast.13, f32[8,4096]{1,0:T(8,128)} %bitcast.14, f32[8,8,512]{2,1,0:T(8,128)} %bitcast.15, f32[1,1]{1,0:T(1,128)S(6)} %copy.8.h_diffusivity, s32[8,4096]{1,0:T(8,128)} %bitcast.16, s32[1,4096]{1,0:T(1,128)} %bitcast.17), custom_call_target="tpu_custom_call" | custom-call | tf_op jit(solution)/shard_map/pallas_call | solution.py:499
  54.0 0.0 copy-done
  54.0 0.7 %fusion.1 = f32[1,1,8,4096]{3,2,1,0:T(8,128)} fusion(f32[8,4096]{1,0:T(8,128)S(1)} %get-tuple-element.7, f32[8,4096]{1,0:T(8,128)S(1)} %get-tuple-element.8, f32[1,1,8,4096]{3,2,1,0:T(8,128)S(1)} %copy-done), kind=kLoop, calls=%fused_computation.2 | loop fusion | flops 65536 | bytes 524288 | tf_op jit(solution)/shard_map/broadcast_in_dim | solution.py:563
Async XLA Ops:
  0.7 53.3 %copy-start = (f32[1,1,8,4096]{3,2,1,0:T(8,128)S(1)}, f32[1,1,8,4096]{3,2,1,0:T(8,128)}, u32[]{:S(2)}) copy-start(f32[1,1,8,4096]{3,2,1,0:T(8,128)} %param.13) | copy-start | bytes 393220

commit v10 on v9

--- a/solution.py
+++ b/solution.py
@@ -138,8 +138,8 @@
     background, norm_factor, v_diffusivity, h_diffusivity, sea_mask, fold_order,
     solved_out, other_out,
     bg, nf, vd, mask_in, fold_in, scaled, rhs, solved, inverse, below, upper,
-    field, quarter_mask, packed_mask, masked, v_chain, p_chain, r_chain, masked_p, masked_r, p_own, r_own,
-    partner_row, partner_lane, lines, folded_p, folded_r, message, received, result,
+    field, quarter_mask, packed_mask, masked, v_chain, v_more, second_basis,
+    partner_row, partner_lane, lines, folded_p, message, received, result,
     load_sem, there_send, there_recv, back_send, back_recv,
     halo_send, halo_recv, mask_send, mask_recv, sum_send, sum_recv, last_send, last_recv, last_local,
 ):
@@ -386,52 +386,53 @@
     pl.when(tile < top - 1)(functools.partial(first_chain, "other"))
     received[0, tile] = message[0]
     reduce_over_tiles(0)
+
+    def more_chain(at_top):
+        source = v_chain[-1]
+        for j in range(second):
+            if at_top:
+                fold(source, 15 if j == 0 else 7, folded_p)
+            operator(
+                source, v_more[j], packed_mask, columns, SHIFTS[j], 8 if j == second - 1 else 16,
+                24 if j == 0 else 16, pack=j == 0, folded=(folded_p, 7) if at_top else None,
+            )
+            source = v_more[j]
+
+    pl.when(is_top)(functools.partial(more_chain, True))
+    pl.when(jnp.logical_not(is_top))(functools.partial(more_chain, False))
+    strip_rows = slice(0, 8)
+    v_basis = [of(field, OWN, 0)] + [of(v, OWN, PAD) for v in v_chain] + [of(v, strip_rows, PAD) for v in v_more]
+
     diffusivity = h_diffusivity[0, 0]
     x_first, r_next, d_next = coefficient_cg(sum_over_tiles(0), (first + 1,), diffusivity, first, False)
 
-    def next_round(block, carry):
+    all_shifts = SHIFTS[:first] + SHIFTS[:second]
+
+    def chain_numbers(numbers, length):
+        chain = [numbers]
+        for j in range(length):
+            parts = {}
+            for i, value in chain[-1].items():
+                parts.setdefault(i + 1, []).append(value)
+                if all_shifts[i] != SHIFTS[j]:
+                    parts.setdefault(i, []).append((0.25 * (all_shifts[i] - SHIFTS[j])) * value)
+            chain.append({i: sum(terms) for i, terms in sorted(parts.items())})
+        return chain
+
+    numbers = chain_numbers(d_next, second) + chain_numbers(r_next, second - 1)
+    basis = [of(one, strip_rows, 0) for one in second_basis]
+
+    def combine(block, carry):
         at = pl.multiple_of(block * 128, 128)
-        rows = slice(0, 24)
-        held = [field[rows, pl.ds(at, 128)]] + [v[rows, pl.ds(at + PAD, 128)] for v in v_chain]
-        mask = 4.0 * quarter_mask[rows, pl.ds(at, 128)]
-        for masked_one, own, numbers in ((masked_r, r_own, r_next), (masked_p, p_own, d_next)):
-            tall = [jnp.concatenate([numbers[j]] * 3, axis=0) for j in numbers]
-            value = tree_sum(number * held[j] for number, j in zip(tall, numbers))
-            masked_one[:, pl.ds(at + PAD, 128)] = mask * value
-            own[:, pl.ds(at, 128)] = value[8:16]
+        held = [v(block) for v in v_basis]
+        for one, terms in zip(second_basis, numbers):
+            one[:, pl.ds(at, 128)] = tree_sum(terms[i] * held[i] for i in terms)
         return carry
 
-    lax.fori_loop(0, blocks, next_round, 0, unroll=True)
-    wrap(masked_r, 24, columns)
-    wrap(masked_p, 24, columns)
-
-    strip_rows = slice(0, 8)
-    p_basis = [of(p_own, strip_rows, 0)] + [of(p, strip_rows, PAD) for p in p_chain]
-    r_basis = [of(r_own, strip_rows, 0)] + [of(r, strip_rows, PAD) for r in r_chain]
-
-    def second_chains(at_top):
-        sources = [masked_p, masked_r]
-        for j in range(second):
-            work = [(sources[0], p_chain[j], folded_p, 8 if j == second - 1 else 16)]
-            if j < second - 1:
-                work.append((sources[1], r_chain[j], folded_r, 8 if j == second - 2 else 16))
-            if at_top:
-                for source, _, folded, _ in work:
-                    fold(source, 15 if j == 0 else 7, folded)
-            for source, target, folded, rows in work:
-                operator(
-                    source, target, packed_mask, columns, SHIFTS[j], rows, 24 if j == 0 else 16,
-                    pack=j == 0, folded=(folded, 7) if at_top else None,
-                )
-            sources = [target for _, target, _, _ in work]
-        message[1] = gram_message(p_basis + r_basis, pairs_of((second + 1, second), True), columns)
-
-    pl.when(is_top)(functools.partial(second_chains, True))
-    pl.when(jnp.logical_not(is_top))(functools.partial(second_chains, False))
+    lax.fori_loop(0, blocks, combine, 0, unroll=True)
+    message[1] = gram_message(basis, pairs_of((second + 1, second), True), columns)
     received[1, tile] = message[1]
     reduce_over_tiles(1)
-    v_basis = [of(field, OWN, 0)] + [of(v, OWN, PAD) for v in v_chain]
-
     def part_one(block, carry):
         at = pl.multiple_of(block * 128, 128)
         result[:, pl.ds(at, 128)] = tree_sum(x_first[j] * v_basis[j](block) for j in x_first)
@@ -440,7 +441,6 @@
     lax.fori_loop(0, blocks, part_one, 0, unroll=True)
     x_second, _, _ = coefficient_cg(sum_over_tiles(1), (second + 1, second), diffusivity, second, True)
 
-    basis = p_basis + r_basis
     pieces = 4
     width = columns // pieces
     for piece in range(pieces):
@@ -521,15 +521,10 @@
             padded(32),
             [padded(32 if j == 0 else 24) for j in range(first)],
             [padded(16)] * second,
-            [padded(16)] * (second - 1),
-            padded(24),
-            padded(24),
-            vmem((rows, columns), f32),
-            vmem((rows, columns), f32),
+            [vmem((rows, columns), f32)] * (2 * second + 1),
             vmem((blocks, 128), jnp.int32),
             vmem((blocks, 128), jnp.int32),
             vmem((blocks, 8, 128), f32),
-            vmem((blocks, 128), f32),
             vmem((blocks, 128), f32),
             vmem((2, 1, 128), f32),
             vmem((2, tiles, 1, 128), f32),

time: 54.8 us -> 53.1 us (0.969)
  the two profiles are of different devices: /device:TPU:8 before, /device:TPU:64 now
where the time goes in v10:
time: 53.1 us; the launch traced here: 53 us
  Pallas kernels  51.6 us (97%)
  other arithmetic  0.68 us (1%)
  between operations  0.68 us (1%)
    pallas_call x1, Pallas kernels, per_device(): pl.pallas_call(kernel, out_shape=(strip, strip), in_specs=[pl.BlockSpec(m...  51.6 us

profile of v10, /device:TPU:64, one launch (start us, length us, event | category | flops | bytes accessed | tf_op | source)
XLA Modules:
  0.0 53.0 jit_solution(5723417937495974889)
XLA Ops:
  0.7 0.0 copy-start
  0.7 51.6 %shard_map.73 = (f32[8,4096]{1,0:T(8,128)S(1)}, f32[8,4096]{1,0:T(8,128)S(1)}) custom-call(f32[8,4096]{1,0:T(8,128)} %bitcast.13, f32[8,4096]{1,0:T(8,128)} %bitcast.14, f32[8,8,512]{2,1,0:T(8,128)} %bitcast.15, f32[1,1]{1,0:T(1,128)S(6)} %copy.8.h_diffusivity, s32[8,4096]{1,0:T(8,128)} %bitcast.16, s32[1,4096]{1,0:T(1,128)} %bitcast.17), custom_call_target="tpu_custom_call" | custom-call | tf_op jit(solution)/shard_map/pallas_call | solution.py:499
  52.3 0.0 copy-done
  52.3 0.7 %fusion.1 = f32[1,1,8,4096]{3,2,1,0:T(8,128)} fusion(f32[8,4096]{1,0:T(8,128)S(1)} %get-tuple-element.7, f32[8,4096]{1,0:T(8,128)S(1)} %get-tuple-element.8, f32[1,1,8,4096]{3,2,1,0:T(8,128)S(1)} %copy-done), kind=kLoop, calls=%fused_computation.2 | loop fusion | flops 65536 | bytes 524288 | tf_op jit(solution)/shard_map/broadcast_in_dim | solution.py:558
Async XLA Ops:
  0.7 51.7 %copy-start = (f32[1,1,8,4096]{3,2,1,0:T(8,128)S(1)}, f32[1,1,8,4096]{3,2,1,0:T(8,128)}, u32[]{:S(2)}) copy-start(f32[1,1,8,4096]{3,2,1,0:T(8,128)} %param.13) | copy-start | bytes 393220

commit v11 on v10

--- a/solution.py
+++ b/solution.py
@@ -157,7 +157,7 @@
             ((background, bg), (norm_factor, nf), (sea_mask, mask_in), (v_diffusivity, vd), (fold_order, fold_in))
         )
     ]
-    for load in loads:
+    for load in loads[:2]:
         load.start()
     barrier = pltpu.get_barrier_semaphore()
     bits = (lax.rem(lev, 2), lax.rem(lev // 2, 2), lev // 4)
@@ -177,11 +177,11 @@
         pl.semaphore_signal(barrier, inc=1, device_id={"lev": peers[d]}, device_id_type=MESH)
     pl.semaphore_signal(barrier, inc=1, device_id={"var": 1 - var}, device_id_type=MESH)
     lax.fori_loop(1, tiles, greet_tile, 0, unroll=True)
+    for load in loads[2:]:
+        load.start()
     loads[0].wait()
     loads[1].wait()
     scaled[...] = nf[...] * bg[...]
-    loads[2].wait()
-    quarter_mask[OWN, :] = 0.25 * mask_in[...].astype(f32)
     pl.semaphore_wait(barrier, (levels - 1) + (tiles - 1) + 1)
 
     for d in reversed(range(1, levels)):
@@ -222,6 +222,8 @@
                 at = slice(land, land + high - low) if receive else slice(low, high)
                 pltpu.make_async_copy(buffer.at[at, :], buffer.at[at, :], sem.at[side]).wait()
 
+    loads[2].wait()
+    quarter_mask[OWN, :] = 0.25 * mask_in[...].astype(f32)
     halo_copies(quarter_mask, mask_send, mask_recv, 0, columns)
     for low, high, land, distance in sides:
 
@@ -341,9 +343,7 @@
                 folded, rows = (folded_p, 15), 16
             elif strip == "next" and j < 2:
                 fold(source, 23, folded_p)
-                for block in range(blocks):
-                    at = PAD + block * 128
-                    source[24:25, at : at + 128] = folded_p[block : block + 1, :]
+                folded = (folded_p, 23)
             if j == 0:
                 rows = 32
             operator(

time: 53.1 us -> 53.1 us (level)
  the two profiles are of different devices: /device:TPU:64 before, /device:TPU:8 now
where the time goes in v11:
time: 53.1 us; the launch traced here: 53 us
  Pallas kernels  51.6 us (97%)
  other arithmetic  0.68 us (1%)
  between operations  0.68 us (1%)
    pallas_call x1, Pallas kernels, per_device(): pl.pallas_call(kernel, out_shape=(strip, strip), in_specs=[pl.BlockSpec(m...  51.6 us

profile of v11, /device:TPU:8, one launch (start us, length us, event | category | flops | bytes accessed | tf_op | source)
XLA Modules:
  0.0 53.0 jit_solution(18352727508501035100)
XLA Ops:
  0.7 0.0 copy-start
  0.7 51.6 %shard_map.73 = (f32[8,4096]{1,0:T(8,128)S(1)}, f32[8,4096]{1,0:T(8,128)S(1)}) custom-call(f32[8,4096]{1,0:T(8,128)} %bitcast.13, f32[8,4096]{1,0:T(8,128)} %bitcast.14, f32[8,8,512]{2,1,0:T(8,128)} %bitcast.15, f32[1,1]{1,0:T(1,128)S(6)} %copy.8.h_diffusivity, s32[8,4096]{1,0:T(8,128)} %bitcast.16, s32[1,4096]{1,0:T(1,128)} %bitcast.17), custom_call_target="tpu_custom_call" | custom-call | tf_op jit(solution)/shard_map/pallas_call | solution.py:499
  52.3 0.0 copy-done
  52.3 0.7 %fusion.1 = f32[1,1,8,4096]{3,2,1,0:T(8,128)} fusion(f32[8,4096]{1,0:T(8,128)S(1)} %get-tuple-element.7, f32[8,4096]{1,0:T(8,128)S(1)} %get-tuple-element.8, f32[1,1,8,4096]{3,2,1,0:T(8,128)S(1)} %copy-done), kind=kLoop, calls=%fused_computation.2 | loop fusion | flops 65536 | bytes 524288 | tf_op jit(solution)/shard_map/broadcast_in_dim | solution.py:558
Async XLA Ops:
  0.7 51.6 %copy-start = (f32[1,1,8,4096]{3,2,1,0:T(8,128)S(1)}, f32[1,1,8,4096]{3,2,1,0:T(8,128)}, u32[]{:S(2)}) copy-start(f32[1,1,8,4096]{3,2,1,0:T(8,128)} %param.13) | copy-start | bytes 393220

commit v12 on v11

--- a/solution.py
+++ b/solution.py
@@ -35,7 +35,8 @@
         group = pairs[at : at + 28]
         used = sorted({i for pair in group for i in pair})
 
-        def body(block, sums, group=group, used=used):
+        def body(step, sums, group=group, used=used):
+            block = lax.rem(step + 8, columns // 128)
             held = {i: vectors[i](block) for i in used}
             return tuple(total + held[i] * held[j] for total, (i, j) in zip(sums, group))
 
@@ -95,14 +96,17 @@
     return jnp.concatenate([tall[8:16], jnp.where(upper_half, tall[16:24], tall[0:8])], axis=0)
 
 
-def operator(source, target, quarter_mask, columns, shift, rows, loaded, pack=False, folded=None, group=8):
+def operator(source, target, quarter_mask, columns, shift, rows, loaded, odd, pack=False, folded=None, group=8):
     lane = lax.broadcasted_iota(jnp.int32, (rows, 128), 1)
     if folded is not None:
         line, last_row = folded
         is_last = lax.broadcasted_iota(jnp.int32, (rows, 128), 0) == last_row
     cut = packed if pack else lambda value: value[0:rows]
 
-    def body(chunk, carry):
+    steps = columns // (group * 128)
+
+    def body(step, carry):
+        chunk = lax.rem(steps + 2 - step, steps) if odd else lax.rem(step + 1, steps)
         at = pl.multiple_of(chunk * (group * 128), 128)
         held, ahead, behind = {}, {}, {}
         for k in range(group + 2):
@@ -125,7 +129,7 @@
             target[0:rows, pl.ds(at + 128 * (k - 1), 128)] = value
         return carry
 
-    lax.fori_loop(0, columns // (group * 128), body, 0, unroll=True)
+    lax.fori_loop(0, steps, body, 0, unroll=True)
     wrap(target, rows, columns)
 
 
@@ -347,7 +351,7 @@
             if j == 0:
                 rows = 32
             operator(
-                source, v_chain[j], quarter_mask, columns, SHIFTS[j], rows, 32 if j < 2 else rows, folded=folded
+                source, v_chain[j], quarter_mask, columns, SHIFTS[j], rows, 32 if j < 2 else rows, j % 2, folded=folded
             )
             source = v_chain[j]
         message[0] = gram_message([of(field, OWN, 0)] + [of(v, OWN, PAD) for v in v_chain], pairs_of((first + 1,), False), columns)
@@ -394,7 +398,7 @@
                 fold(source, 15 if j == 0 else 7, folded_p)
             operator(
                 source, v_more[j], packed_mask, columns, SHIFTS[j], 8 if j == second - 1 else 16,
-                24 if j == 0 else 16, pack=j == 0, folded=(folded_p, 7) if at_top else None,
+                24 if j == 0 else 16, 1 - j % 2, pack=j == 0, folded=(folded_p, 7) if at_top else None,
             )
             source = v_more[j]
 

time: 53.1 us -> 52.9 us (level)
  the two profiles are of different devices: /device:TPU:8 before, /device:TPU:64 now
where the time goes in v12:
time: 52.9 us; the launch traced here: 52.8 us
  Pallas kernels  51.4 us (97%)
  other arithmetic  0.68 us (1%)
  between operations  0.68 us (1%)
    pallas_call x1, Pallas kernels, per_device(): pl.pallas_call(kernel, out_shape=(strip, strip), in_specs=[pl.BlockSpec(m...  51.4 us

profile of v12, /device:TPU:64, one launch (start us, length us, event | category | flops | bytes accessed | tf_op | source)
XLA Modules:
  0.0 52.8 jit_solution(469766903400525635)
XLA Ops:
  0.7 0.0 copy-start
  0.7 51.4 %shard_map.73 = (f32[8,4096]{1,0:T(8,128)S(1)}, f32[8,4096]{1,0:T(8,128)S(1)}) custom-call(f32[8,4096]{1,0:T(8,128)} %bitcast.13, f32[8,4096]{1,0:T(8,128)} %bitcast.14, f32[8,8,512]{2,1,0:T(8,128)} %bitcast.15, f32[1,1]{1,0:T(1,128)S(6)} %copy.8.h_diffusivity, s32[8,4096]{1,0:T(8,128)} %bitcast.16, s32[1,4096]{1,0:T(1,128)} %bitcast.17), custom_call_target="tpu_custom_call" | custom-call | tf_op jit(solution)/shard_map/pallas_call | solution.py:503
  52.1 0.0 copy-done
  52.1 0.7 %fusion.1 = f32[1,1,8,4096]{3,2,1,0:T(8,128)} fusion(f32[8,4096]{1,0:T(8,128)S(1)} %get-tuple-element.7, f32[8,4096]{1,0:T(8,128)S(1)} %get-tuple-element.8, f32[1,1,8,4096]{3,2,1,0:T(8,128)S(1)} %copy-done), kind=kLoop, calls=%fused_computation.2 | loop fusion | flops 65536 | bytes 524288 | tf_op jit(solution)/shard_map/broadcast_in_dim | solution.py:562
Async XLA Ops:
  0.7 51.4 %copy-start = (f32[1,1,8,4096]{3,2,1,0:T(8,128)S(1)}, f32[1,1,8,4096]{3,2,1,0:T(8,128)}, u32[]{:S(2)}) copy-start(f32[1,1,8,4096]{3,2,1,0:T(8,128)} %param.13) | copy-start | bytes 393220

commit v13 on v11

--- a/solution.py
+++ b/solution.py
@@ -293,7 +293,9 @@
         at = pl.multiple_of(peers[d] * part, part)
         here = field.at[OWN, pl.ds(at, part)]
         pltpu.make_async_copy(here, here, back_recv.at[d]).wait()
-        if d % 2 == 1:
+        if d >= levels - 2:
+            halo_copies(field, halo_send, halo_recv, at, part)
+        elif d % 2 == 1:
             at = pl.multiple_of(peers[d] // 2 * (2 * part), 2 * part)
             halo_copies(field, halo_send, halo_recv, at, 2 * part)
 

time: 53.1 us -> 53.1 us (level)
  no operation moved by 1% of the time
where the time goes in v13:
time: 53.1 us; the launch traced here: 53 us
  Pallas kernels  51.7 us (97%)
  other arithmetic  0.68 us (1%)
  between operations  0.68 us (1%)
    pallas_call x1, Pallas kernels, per_device(): pl.pallas_call(kernel, out_shape=(strip, strip), in_specs=[pl.BlockSpec(m...  51.7 us

profile of v13, /device:TPU:8, one launch (start us, length us, event | category | flops | bytes accessed | tf_op | source)
XLA Modules:
  0.0 53.0 jit_solution(14951972942315721376)
XLA Ops:
  0.7 0.0 copy-start
  0.7 51.7 %shard_map.73 = (f32[8,4096]{1,0:T(8,128)S(1)}, f32[8,4096]{1,0:T(8,128)S(1)}) custom-call(f32[8,4096]{1,0:T(8,128)} %bitcast.13, f32[8,4096]{1,0:T(8,128)} %bitcast.14, f32[8,8,512]{2,1,0:T(8,128)} %bitcast.15, f32[1,1]{1,0:T(1,128)S(6)} %copy.8.h_diffusivity, s32[8,4096]{1,0:T(8,128)} %bitcast.16, s32[1,4096]{1,0:T(1,128)} %bitcast.17), custom_call_target="tpu_custom_call" | custom-call | tf_op jit(solution)/shard_map/pallas_call | solution.py:501
  52.3 0.0 copy-done
  52.3 0.7 %fusion.1 = f32[1,1,8,4096]{3,2,1,0:T(8,128)} fusion(f32[8,4096]{1,0:T(8,128)S(1)} %get-tuple-element.7, f32[8,4096]{1,0:T(8,128)S(1)} %get-tuple-element.8, f32[1,1,8,4096]{3,2,1,0:T(8,128)S(1)} %copy-done), kind=kLoop, calls=%fused_computation.2 | loop fusion | flops 65536 | bytes 524288 | tf_op jit(solution)/shard_map/broadcast_in_dim | solution.py:560
Async XLA Ops:
  0.7 51.7 %copy-start = (f32[1,1,8,4096]{3,2,1,0:T(8,128)S(1)}, f32[1,1,8,4096]{3,2,1,0:T(8,128)}, u32[]{:S(2)}) copy-start(f32[1,1,8,4096]{3,2,1,0:T(8,128)} %param.13) | copy-start | bytes 393220
